TPU v7x, 32 devices: a whole 2x2x4 slice. The times are simulated.
32 devices in a mesh: lon: 16 (over z, y, x), lat: 2 (over core).
Axes of the slice: x: 2, y: 2, z: 4, core: 2. Of those that a mesh axis runs over, the one named last changes fastest.
Arguments:
- inputs: bfloat16 [16, 512, 256], P('lat', 'lon'), may hold values from -6 to 6
- psi_raw: float32 [4, 16, 3, 257], P(None, 'lat'), may hold values from -6 to 6
- widths: int32 [16], P('lat'), may hold values from 1 to 4, as said below
- w_group: bfloat16 [4, 4, 256], replicated, may hold values from -1.5 to 1.5
- w_mix: bfloat16 [256, 256], replicated, may hold values from -0.375 to 0.375
- grad_out: bfloat16 [16, 512, 256], P('lat', 'lon'), may hold values from -6 to 6
Outputs:
- outputs: bfloat16 [16, 512, 256], P('lat', 'lon')
- grad_in: bfloat16 [16, 512, 256], P('lat', 'lon')
Inputs may be any that keep to these rules, and one draw needn't show every extreme that they name: `widths`: let d be a row's distance to the nearer pole (min(i, 15 - i)). A row's width is at most min(4, max(1, 2 * 4 // (d + 1)) + 1); the row nearest each pole has width 4.
All inputs are finite; a program needn't handle non-finite values.
Results may differ from a plain program's by a relative error of at most 0.011.
Values may be sent and summed in bfloat16 or wider, within the bound.
No kernel may reach another device: no remote copies, remote signals or barrier semaphores. Data moves between devices by JAX's collectives and lax.ppermute only.
A program may use at most 192 MiB of HBM per device.

v0:
```python
from functools import partial

import jax
import jax.numpy as jnp
from jax import lax
from jax.experimental import pallas as pl
from jax.experimental.pallas import tpu as pltpu
from jax.sharding import PartitionSpec as P

GROUP = 4
SMAX = 4


LANES = 128
BF16 = jnp.bfloat16
ALONG = (((1,), (1,)), ((), ()))
SMALL = pltpu.CompilerParams(vmem_limit_bytes=4 * 2**20)
LARGE = pltpu.CompilerParams(vmem_limit_bytes=12 * 2**20)


def width_bound(row, row_total):
    pole = min(row, row_total - 1 - row)
    return min(SMAX, max(1, 2 * SMAX // (pole + 1)) + 1)


def reaches(row_count, bands):
    total = row_count * bands
    bound = [width_bound(row, total) for row in range(total)]
    near = [max(bound[max(0, row - 1) : row + 2]) for row in range(total)]
    return bound, near


def iota(shape, axis):
    return lax.broadcasted_iota(jnp.int32, shape, axis)


def turned_by_identity(values):
    count = values.shape[1]
    unit = jnp.where(iota((count, count), 0) == iota((count, count), 1), 1.0, 0.0).astype(BF16)
    return lax.dot_general(unit, values, ALONG, preferred_element_type=jnp.float32).astype(BF16)


def transpose_kernel(x_ref, o_ref):
    o_ref[...] = turned_by_identity(x_ref[...])


def transposed(values):
    return pl.pallas_call(
        transpose_kernel,
        out_shape=jax.ShapeDtypeStruct(values.shape[::-1], values.dtype),
        compiler_params=SMALL,
    )(values)


def enter_kernel(lon_dev, w_ref, x_ref, p_ref, o_ref, f_ref):
    o_ref[...] = turned_by_identity(x_ref[...])
    kernels, taps, rows, cells = p_ref.shape
    shape = (rows, LANES)
    line, lane = iota(shape, 0), iota(shape, 1)
    reach = jnp.zeros(shape, jnp.int32)
    for row in range(rows):
        reach = jnp.where(line == row, w_ref[row] * lon_dev, reach)
    scale = lax.rsqrt(3.0 * (2.0 * reach.astype(jnp.float32) + 1.0))
    for tile in range(3):
        offset = lane + (tile * LANES - SMAX * lon_dev)
        keep = jnp.where(jnp.abs(offset) <= reach, scale, 0.0)
        for k in range(kernels):
            for tap in range(taps):
                if tile < 2:
                    values = p_ref[k, tap, :, pl.ds(tile * LANES, LANES)]
                else:
                    values = p_ref[k, tap, :, pl.ds(cells - 1, 1)]
                    values = jnp.where(lane == 0, values, 0.0)
                f_ref[k, tap, :, pl.ds(tile * LANES, LANES)] = (
                    (values * keep).astype(BF16).astype(jnp.float32)
                )


def collect(bands, merged, backward, filter_refs, f):
    if merged:
        band = lax.axis_index("lat")
        f[band] = filter_refs[0][...]
        f[1 - band] = filter_refs[1][...]
    else:
        for segment, ref in enumerate(filter_refs):
            f[segment] = ref[...]
    if backward:
        segments, kernels, taps, lines, width = f.shape
        shape = (width, width)
        mirror = jnp.where(iota(shape, 0) + iota(shape, 1) == 2 * LANES, 1.0, 0.0).astype(BF16)
        for segment in range(segments):
            values = f[segment].reshape(kernels * taps * lines, width).astype(BF16)
            values = jnp.dot(values, mirror, preferred_element_type=jnp.float32)
            f[segment] = values.reshape(kernels, taps, lines, width)


def lay_toeplitz(rows, wide, lon_dev, merged, backward, f, t_ref, e_ref):
    segments, kernels, _, held, _ = f.shape
    shape = (lon_dev, LANES)
    lane, line = iota(shape, 1), iota(shape, 0)
    upper = lane >= line
    corner = lane == line
    for row in range(rows):
        for tap in range(3):
            source, column = (row + tap - 1, 2 - tap) if backward else (row, tap)
            source += 0 if merged else held
            segment, inner = divmod(source, held)
            present = 0 <= segment < segments
            for k in range(kernels):
                here = pl.ds(k * lon_dev, lon_dev)

                def turned(tile):
                    values = f[segment, k, column, pl.ds(inner, 1), pl.ds(tile * LANES, LANES)]
                    values = jnp.broadcast_to(values, shape)
                    return pltpu.roll(values, 0, 1, stride=1, stride_axis=0)

                if present:
                    first, second = turned(0), turned(1)
                    parts = [jnp.where(upper, first, 0.0), jnp.where(upper, second, first)]
                else:
                    parts = [jnp.zeros(shape, jnp.float32)] * 2
                for i, part in enumerate(parts):
                    t_ref[row, here, pl.ds((tap * 2 + i) * LANES, LANES)] = part.astype(BF16)
                if row in wide:
                    last = parts[0]
                    if present:
                        last = jnp.where(corner, turned(2), jnp.where(upper, 0.0, second))
                    at = pl.ds(tap * LANES, LANES)
                    e_ref[wide.index(row), here, at] = last.astype(BF16)


def mixer_of(everyone, share, backward, w_ref, height):
    kernels, group, channels = w_ref.shape
    first = lax.axis_index(everyone[0])
    for axis in everyone[1:]:
        first = first * lax.axis_size(axis) + lax.axis_index(axis)
    shape = (channels, height)
    chosen = iota(shape, 0) == first * share + iota(shape, 1) % share
    weights = jnp.concatenate([w_ref[k].astype(jnp.float32) for k in range(kernels)], axis=0)
    weights = jnp.dot(
        weights.astype(BF16),
        jnp.where(chosen, 1.0, 0.0).astype(BF16),
        preferred_element_type=jnp.float32,
    )
    if backward:
        spread = [
            jnp.concatenate([weights[k * group : (k + 1) * group]] * (height // group), axis=0)
            for k in range(kernels)
        ]
        spread = jnp.concatenate(spread, axis=1)
    else:
        shape = (kernels * group, kernels * height)
        line, lane = iota(shape, 0), iota(shape, 1)
        pick = line == (lane // height) * group + lane % group
        spread = lax.dot_general(
            weights.astype(BF16),
            jnp.where(pick, 1.0, 0.0).astype(BF16),
            (((0,), (0,)), ((), ())),
            preferred_element_type=jnp.float32,
        )
    shape = (height, kernels * height)
    same = iota(shape, 0) // group == (iota(shape, 1) % height) // group
    return jnp.where(same, spread, 0.0).astype(BF16)


def conv_kernel(
    table, bands, lon_dev, merged, everyone, share, backward, w_ref, own_ref, *refs
):
    count = 2 if merged else 3
    filter_refs, refs = refs[:count], refs[count:]
    *halo_refs, o_ref, f, t_ref, e_ref, xs, z_ref = refs
    segments, height, cells = own_ref.shape
    rows = len(table)
    held = rows // segments
    kernels = f.shape[1]
    wide = [row for row, reach in enumerate(table) if reach == SMAX]
    collect(bands, merged, backward, filter_refs, f)
    lay_toeplitz(rows, wide, lon_dev, merged, backward, f, t_ref, e_ref)

    def put(values, first):
        values = values.T.astype(jnp.float32)
        count = values.shape[0] // lon_dev
        for shard in range(-SMAX, SMAX + 1):
            turned = pltpu.roll(values, -shard * share % height, 1) if shard else values
            at = pl.ds((shard + SMAX) * lon_dev, lon_dev)
            xs[pl.ds(first + 1, count), at, :] = turned.astype(BF16).reshape(
                count, lon_dev, height
            )

    per_tile = LANES // lon_dev
    blank = jnp.zeros(xs.shape[1:], BF16)
    if halo_refs:
        band = lax.axis_index("lat")
        above = halo_refs[0][:, pl.ds(cells - LANES, LANES)]
        put(above, 0)
        edge = xs[per_tile].astype(jnp.float32)
        xs[0] = jnp.where(band > 0, edge, 0.0).astype(BF16)
        put(halo_refs[1][:, pl.ds(0, LANES)], 0)
        edge = xs[1].astype(jnp.float32)
        xs[rows + 1] = jnp.where(band < bands - 1, edge, 0.0).astype(BF16)
    else:
        xs[0] = blank
        xs[rows + 1] = blank
    for segment in range(segments):
        put(own_ref[segment], segment * held)
    span = 2 * LANES
    for row in range(rows):
        window = xs[row : row + 3, :span, :].reshape(3 * span, height)
        total = jnp.dot(t_ref[row], window, preferred_element_type=jnp.float32)
        if row in wide:
            beyond = []
            for tap in range(3):
                beyond += [xs[row + tap, span:, :], blank[: LANES - lon_dev]]
            total += jnp.dot(
                e_ref[wide.index(row)],
                jnp.concatenate(beyond, axis=0),
                preferred_element_type=jnp.float32,
            )
        total = total.astype(BF16)
        for k in range(kernels):
            z_ref[pl.ds(row * lon_dev, lon_dev), pl.ds(k * height, height)] = total[
                k * lon_dev : (k + 1) * lon_dev
            ]
    mixer = mixer_of(everyone, share, backward, w_ref, height)
    for segment in range(segments):
        part = z_ref[pl.ds(segment * cells, cells), :]
        mixed = lax.dot_general(mixer, part, ALONG, preferred_element_type=jnp.float32)
        o_ref[segment] = mixed.astype(o_ref.dtype)


def dense_kernel(m_ref, w_ref, g_ref, o_ref, d_ref):
    mixed_in = turned_by_identity(m_ref[...])
    pre = jnp.dot(mixed_in, w_ref[...], preferred_element_type=jnp.float32)
    slope = 0.7978845608028654
    square = pre * pre
    bent = jnp.tanh(slope * (pre + 0.044715 * (square * pre)))
    half = 0.5 * (1.0 + bent)
    o_ref[...] = (pre * half).astype(o_ref.dtype)
    rise = half + 0.5 * pre * (1.0 - bent * bent) * (slope * (1.0 + 3.0 * 0.044715 * square))
    grad_pre = (g_ref[...].astype(jnp.float32) * rise).astype(BF16)
    d_ref[...] = lax.dot_general(
        w_ref[...], grad_pre, ALONG, preferred_element_type=jnp.float32
    ).astype(d_ref.dtype)


def from_bands(values):
    count = lax.axis_size("lat")
    up = [(i, i + 1) for i in range(count - 1)]
    down = [(j, i) for i, j in up]
    return [lax.ppermute(values, "lat", up), lax.ppermute(values, "lat", down)]


def body(inputs, psi_raw, widths, w_group, w_mix, grad_out):
    row_count, lon_dev, channels = inputs.shape
    kernels = psi_raw.shape[0]
    blocks, bands = lax.axis_size("lon"), lax.axis_size("lat")
    cells = row_count * lon_dev
    merged = bands == 2 and channels % (2 * GROUP * bands * blocks) == 0
    everyone = ("lat", "lon") if merged else ("lon",)
    segments = bands if merged else 1
    share = channels // (segments * blocks)
    height = blocks * share
    rows = segments * row_count
    tables = [
        tuple(max(table[row::rows]) for row in range(rows))
        for table in reaches(row_count, bands)
    ]
    square = jax.ShapeDtypeStruct((channels, cells), BF16)

    def exchange(values):
        parted = values.reshape(segments * blocks, share, cells)
        return lax.all_to_all(parted, everyone, 0, 0)

    turned, own_filters = pl.pallas_call(
        partial(enter_kernel, lon_dev),
        out_shape=(
            square,
            jax.ShapeDtypeStruct((kernels, 3, row_count, 3 * LANES), jnp.float32),
        ),
        in_specs=[
            pl.BlockSpec(memory_space=pltpu.SMEM),
            pl.BlockSpec(memory_space=pltpu.VMEM),
            pl.BlockSpec(memory_space=pltpu.VMEM),
        ],
    )(widths, inputs.reshape(cells, channels), psi_raw.transpose(0, 2, 1, 3))
    columns = exchange(turned)
    if merged:
        filters = [own_filters, lax.ppermute(own_filters, "lat", [(0, 1), (1, 0)])]
    else:
        above, below = from_bands(own_filters)
        filters = [above, own_filters, below]
    pool = (bands if merged else 3, *own_filters.shape)

    def convolve(values, backward):
        values = values.reshape(segments, height, cells)
        halo = [] if merged else from_bands(values[0])
        return pl.pallas_call(
            partial(
                conv_kernel, tables[backward], bands, lon_dev, merged, everyone, share,
                bool(backward),
            ),
            out_shape=jax.ShapeDtypeStruct(values.shape, BF16),
            scratch_shapes=[
                pltpu.VMEM(pool, jnp.float32),
                pltpu.VMEM((rows, kernels * lon_dev, 6 * LANES), BF16),
                pltpu.VMEM((tables[backward].count(SMAX), kernels * lon_dev, 3 * LANES), BF16),
                pltpu.VMEM((rows + 2, (2 * SMAX + 1) * lon_dev, height), BF16),
                pltpu.VMEM((rows * lon_dev, kernels * height), BF16),
            ],
            compiler_params=LARGE,
        )(w_group, values, *filters, *halo)

    mixed_in = exchange(convolve(columns, 0))
    outputs, grad_mixed = pl.pallas_call(
        dense_kernel,
        out_shape=(jax.ShapeDtypeStruct((cells, channels), BF16), square),
        compiler_params=SMALL,
    )(mixed_in.reshape(channels, cells), w_mix, grad_out.reshape(cells, channels))
    grad_in = exchange(convolve(exchange(grad_mixed), 1))
    grad_in = transposed(grad_in.reshape(channels, cells))
    return outputs.reshape(inputs.shape), grad_in.reshape(inputs.shape)


def solution(mesh):
    return jax.shard_map(
        body,
        mesh=mesh,
        in_specs=(
            P("lat", "lon", None),
            P(None, "lat", None, None),
            P("lat"),
            P(),
            P(),
            P("lat", "lon", None),
        ),
        out_specs=(P("lat", "lon", None), P("lat", "lon", None)),
        check_vma=False,
    )
```

profile of v0, /device:TPU:0, one launch (start us, length us, event | category | flops | bytes accessed | tf_op | source)
XLA Modules:
  0.0 53.9 jit_solution(14568444747462486059)
XLA Ops:
  0.6 1.9 %shard_map.77 = (bf16[256,256]{1,0:T(8,128)(2,1)}, f32[4,3,8,384]{3,2,1,0:T(8,128)}) custom-call(s32[8]{0:T(128)} %w_ref.4, bf16[256,256]{1,0:T(8,128)(2,1)} %bitcast.22, f32[4,3,8,257]{3,2,1,0:T(8,128)} %bitcast.21), custom_call_target="tpu_custom_call" | custom-call | tf_op jit(solution)/shard_map/pallas_call | solution.py:274
  2.5 0.0 copy-start
  2.5 0.0 copy-start.3
  2.5 7.3 %all-to-all-start = ((bf16[32,8,256]{2,1,0:T(8,128)(2,1)}), bf16[32,8,256]{2,1,0:T(8,128)(2,1)S(1)}, u32[]{:S(2)}, u32[]{:S(2)}) async-start(bf16[32,8,256]{2,1,0:T(8,128)(2,1)} %bitcast.23), calls=%async_computation | async-start | bytes 262144 | tf_op jit(solution)/shard_map/all_to_all | solution.py:272
  9.8 0.0 copy-done
  9.8 0.3 collective-permute-start
  10.1 1.1 %collective-permute-done.refs_1_ = f32[4,3,8,384]{3,2,1,0:T(8,128)S(1)} collective-permute-done((f32[4,3,8,384]{3,2,1,0:T(8,128)S(1)}, f32[4,3,8,384]{3,2,1,0:T(8,128)S(1)}, u32[]{:S(2)}, u32[]{:S(2)}) %collective-permute-start) | collective-permute-done | bytes 147488 | tf_op jit(solution)/shard_map/ppermute | solution.py:288
  11.3 6.5 %all-to-all-done = bf16[32,8,256]{2,1,0:T(8,128)(2,1)S(1)} async-done(((bf16[32,8,256]{2,1,0:T(8,128)(2,1)}), bf16[32,8,256]{2,1,0:T(8,128)(2,1)S(1)}, u32[]{:S(2)}, u32[]{:S(2)}) %all-to-all-start) | async-done | bytes 131104 | tf_op jit(solution)/shard_map/all_to_all | solution.py:272
  17.7 0.0 copy-done.3
  17.7 2.1 %shard_map.78 = bf16[2,128,256]{2,1,0:T(8,128)(2,1)S(1)} custom-call(bf16[4,4,256]{2,1,0:T(4,128)(2,1)S(1)} %copy-done.3, bf16[2,128,256]{2,1,0:T(8,128)(2,1)S(1)} %bitcast.13, f32[4,3,8,384]{3,2,1,0:T(8,128)S(1)} %copy-done, f32[4,3,8,384]{3,2,1,0:T(8,128)S(1)} %collective-permute-done.refs_1_), custom_call_target="tpu_custom_call" | custom-call | tf_op jit(solution)/shard_map/pallas_call | solution.py:297
  19.8 0.0 copy-start.1
  19.9 0.0 copy-start.2
  19.9 9.9 %all_to_all.20 = bf16[32,8,256]{2,1,0:T(8,128)(2,1)S(1)} all-to-all(bf16[32,8,256]{2,1,0:T(8,128)(2,1)S(1)} %bitcast.17), channel_id=1, replica_groups=mesh['lon'=16,'lat'=2] {'lat','lon'}, dimensions={0} | all-to-all | bytes 262144 | tf_op jit(solution)/shard_map/all_to_all | solution.py:272
  29.8 0.0 copy-done.1
  29.8 0.0 copy-done.2
  29.8 1.1 %shard_map.79 = (bf16[256,256]{1,0:T(8,128)(2,1)}, bf16[256,256]{1,0:T(8,128)(2,1)S(1)}) custom-call(bf16[256,256]{1,0:T(8,128)(2,1)S(1)} %bitcast.14, bf16[256,256]{1,0:T(8,128)(2,1)S(1)} %copy-done.1, bf16[256,256]{1,0:T(8,128)(2,1)S(1)} %bitcast.19), custom_call_target="tpu_custom_call" | custom-call | tf_op jit(solution)/shard_map/pallas_call | solution.py:314
  30.9 9.9 %all_to_all.21 = bf16[32,8,256]{2,1,0:T(8,128)(2,1)S(1)} all-to-all(bf16[32,8,256]{2,1,0:T(8,128)(2,1)S(1)} %bitcast.20), channel_id=1, replica_groups=mesh['lon'=16,'lat'=2] {'lat','lon'}, dimensions={0} | all-to-all | bytes 262144 | tf_op jit(solution)/shard_map/all_to_all | solution.py:272
  40.8 2.3 %shard_map.80 = bf16[2,128,256]{2,1,0:T(8,128)(2,1)S(1)} custom-call(bf16[4,4,256]{2,1,0:T(4,128)(2,1)S(1)} %copy-done.3, bf16[2,128,256]{2,1,0:T(8,128)(2,1)S(1)} %bitcast.15, f32[4,3,8,384]{3,2,1,0:T(8,128)S(1)} %copy-done, f32[4,3,8,384]{3,2,1,0:T(8,128)S(1)} %collective-permute-done.refs_1_), custom_call_target="tpu_custom_call" | custom-call | tf_op jit(solution)/shard_map/pallas_call | solution.py:297
  43.1 9.9 %all_to_all.22 = bf16[32,8,256]{2,1,0:T(8,128)(2,1)S(1)} all-to-all(bf16[32,8,256]{2,1,0:T(8,128)(2,1)S(1)} %bitcast.16), channel_id=1, replica_groups=mesh['lon'=16,'lat'=2] {'lat','lon'}, dimensions={0} | all-to-all | bytes 262144 | tf_op jit(solution)/shard_map/all_to_all | solution.py:272
  53.0 0.9 %shard_map.81 = bf16[256,256]{1,0:T(8,128)(2,1)} custom-call(bf16[256,256]{1,0:T(8,128)(2,1)S(1)} %bitcast.18), custom_call_target="tpu_custom_call" | custom-call | tf_op jit(solution)/shard_map/pallas_call | solution.py:48
Async XLA Ops:
  2.5 7.3 %copy-start = (f32[4,3,8,384]{3,2,1,0:T(8,128)S(1)}, f32[4,3,8,384]{3,2,1,0:T(8,128)}, u32[]{:S(2)}) copy-start(f32[4,3,8,384]{3,2,1,0:T(8,128)} %get-tuple-element.7.refs_0_) | copy-start | bytes 442372
  2.5 15.2 %copy-start.3 = (bf16[4,4,256]{2,1,0:T(4,128)(2,1)S(1)}, bf16[4,4,256]{2,1,0:T(4,128)(2,1)}, u32[]{:S(2)}) copy-start(bf16[4,4,256]{2,1,0:T(4,128)(2,1)} %w_ref.7) | copy-start | bytes 24580
  2.5 15.2 %all-to-all-start = ((bf16[32,8,256]{2,1,0:T(8,128)(2,1)}), bf16[32,8,256]{2,1,0:T(8,128)(2,1)S(1)}, u32[]{:S(2)}, u32[]{:S(2)}) async-start(bf16[32,8,256]{2,1,0:T(8,128)(2,1)} %bitcast.23), calls=%async_computation | async-start | bytes 262144 | tf_op jit(solution)/shard_map/all_to_all | solution.py:272
  9.8 1.4 %collective-permute-start = (f32[4,3,8,384]{3,2,1,0:T(8,128)S(1)}, f32[4,3,8,384]{3,2,1,0:T(8,128)S(1)}, u32[]{:S(2)}, u32[]{:S(2)}) collective-permute-start(f32[4,3,8,384]{3,2,1,0:T(8,128)S(1)} %copy-done), channel_id=1, source_target_pairs={{0,1},{1,0},{2,3},{3,2},{4,5},{5,4},{6,7},{7,6},{8,9},{9,8},{10,11... | collective-permute-start | bytes 442376 | tf_op jit(solution)/shard_map/ppermute | solution.py:288
  19.8 9.9 %copy-start.1 = (bf16[256,256]{1,0:T(8,128)(2,1)S(1)}, bf16[256,256]{1,0:T(8,128)(2,1)}, u32[]{:S(2)}) copy-start(bf16[256,256]{1,0:T(8,128)(2,1)} %w_ref.6) | copy-start | bytes 393220
  19.9 9.9 %copy-start.2 = (bf16[8,32,256]{2,1,0:T(8,128)(2,1)S(1)}, bf16[8,32,256]{2,1,0:T(8,128)(2,1)}, u32[]{:S(2)}) copy-start(bf16[8,32,256]{2,1,0:T(8,128)(2,1)} %param.11) | copy-start | bytes 393220
where the time goes:
time: 54.1 us; the launch traced here: 53.9 us
  blocking collectives  29.7 us (55%)
  Pallas kernels  8.25 us (15%)
  starting transfers between devices  7.61 us (14%)
  waiting for transfers between devices  7.58 us (14%)
  between operations  0.68 us (1%)
    all_to_all x3, blocking collectives, exchange(): return lax.all_to_all(parted, everyone, 0, 0)  29.7 us
    all_to_all x1, starting transfers between devices, exchange(): return lax.all_to_all(parted, everyone, 0, 0)  7.3 us
    all_to_all x1, waiting for transfers between devices, exchange(): return lax.all_to_all(parted, everyone, 0, 0)  6.46 us
    pallas_call x2, Pallas kernels, convolve(): pl.pallas_call(partial(conv_kernel, tables[backward], bands, lon_dev, mer...  4.37 us
    pallas_call x1, Pallas kernels, body(): pl.pallas_call(partial(enter_kernel, lon_dev), out_shape=(square, jax.Sha...  1.87 us
    pallas_call x1, Pallas kernels, body(): pl.pallas_call(dense_kernel, out_shape=(jax.ShapeDtypeStruct((cells, chan...  1.14 us
    ppermute x1, waiting for transfers between devices, body(): filters = [own_filters, lax.ppermute(own_filters, 'lat', [(0, 1), (1, 0)])]  1.12 us
  transfers between devices with their start and end apart: 2, of which 2 were waited for; matrix products, arithmetic and copies ran while one was open for 0% of the time, Pallas kernels for 0%

commit v1 on v0

--- a/solution.py
+++ b/solution.py
@@ -14,8 +14,7 @@
 LANES = 128
 BF16 = jnp.bfloat16
 ALONG = (((1,), (1,)), ((), ()))
-SMALL = pltpu.CompilerParams(vmem_limit_bytes=4 * 2**20)
-LARGE = pltpu.CompilerParams(vmem_limit_bytes=12 * 2**20)
+SMALL = pltpu.CompilerParams(vmem_limit_bytes=8 * 2**20)
 
 
 def width_bound(row, row_total):
@@ -94,7 +93,16 @@
             f[segment] = values.reshape(kernels, taps, lines, width)
 
 
-def lay_toeplitz(rows, wide, lon_dev, merged, backward, f, t_ref, e_ref):
+def extra_rows(wide):
+    return (len(wide) + 1) // 2
+
+
+def beyond_at(rows, wide, row):
+    place = wide.index(row)
+    return rows + place // 2, place % 2 * 3 * LANES
+
+
+def lay_toeplitz(rows, wide, lon_dev, merged, backward, f, t_ref):
     segments, kernels, _, held, _ = f.shape
     shape = (lon_dev, LANES)
     lane, line = iota(shape, 1), iota(shape, 0)
@@ -125,8 +133,8 @@
                     last = parts[0]
                     if present:
                         last = jnp.where(corner, turned(2), jnp.where(upper, 0.0, second))
-                    at = pl.ds(tap * LANES, LANES)
-                    e_ref[wide.index(row), here, at] = last.astype(BF16)
+                    after, at = beyond_at(rows, wide, row)
+                    t_ref[after, here, pl.ds(at + tap * LANES, LANES)] = last.astype(BF16)
 
 
 def mixer_of(everyone, share, backward, w_ref, height):
@@ -163,19 +171,17 @@
     return jnp.where(same, spread, 0.0).astype(BF16)
 
 
-def conv_kernel(
-    table, bands, lon_dev, merged, everyone, share, backward, w_ref, own_ref, *refs
-):
-    count = 2 if merged else 3
-    filter_refs, refs = refs[:count], refs[count:]
-    *halo_refs, o_ref, f, t_ref, e_ref, xs, z_ref = refs
+def table_kernel(wide, rows, bands, lon_dev, merged, backward, *refs):
+    *filter_refs, t_ref, f = refs
+    collect(bands, merged, backward, filter_refs, f)
+    lay_toeplitz(rows, wide, lon_dev, merged, backward, f, t_ref)
+
+
+def conv_kernel(wide, rows, bands, lon_dev, everyone, share, backward, *refs):
+    w_ref, own_ref, t_ref, *halo_refs, o_ref, xs, z_ref = refs
     segments, height, cells = own_ref.shape
-    rows = len(table)
     held = rows // segments
-    kernels = f.shape[1]
-    wide = [row for row, reach in enumerate(table) if reach == SMAX]
-    collect(bands, merged, backward, filter_refs, f)
-    lay_toeplitz(rows, wide, lon_dev, merged, backward, f, t_ref, e_ref)
+    kernels = w_ref.shape[0]
 
     def put(values, first):
         values = values.T.astype(jnp.float32)
@@ -211,8 +217,9 @@
             beyond = []
             for tap in range(3):
                 beyond += [xs[row + tap, span:, :], blank[: LANES - lon_dev]]
+            after, at = beyond_at(rows, wide, row)
             total += jnp.dot(
-                e_ref[wide.index(row)],
+                t_ref[after, :, pl.ds(at, 3 * LANES)],
                 jnp.concatenate(beyond, axis=0),
                 preferred_element_type=jnp.float32,
             )
@@ -261,8 +268,8 @@
     share = channels // (segments * blocks)
     height = blocks * share
     rows = segments * row_count
-    tables = [
-        tuple(max(table[row::rows]) for row in range(rows))
+    wide = [
+        tuple(row for row in range(rows) if max(table[row::rows]) == SMAX)
         for table in reaches(row_count, bands)
     ]
     square = jax.ShapeDtypeStruct((channels, cells), BF16)
@@ -291,32 +298,40 @@
         filters = [above, own_filters, below]
     pool = (bands if merged else 3, *own_filters.shape)
 
-    def convolve(values, backward):
+    def lay(filters, backward):
+        some = wide[backward]
+        shape = (rows + extra_rows(some), kernels * lon_dev, 6 * LANES)
+        return pl.pallas_call(
+            partial(table_kernel, some, rows, bands, lon_dev, merged, bool(backward)),
+            out_shape=jax.ShapeDtypeStruct(shape, BF16),
+            scratch_shapes=[pltpu.VMEM(pool, jnp.float32)],
+            compiler_params=SMALL,
+        )(*filters)
+
+    def convolve(values, table, backward):
         values = values.reshape(segments, height, cells)
         halo = [] if merged else from_bands(values[0])
         return pl.pallas_call(
             partial(
-                conv_kernel, tables[backward], bands, lon_dev, merged, everyone, share,
-                bool(backward),
+                conv_kernel, wide[backward], rows, bands, lon_dev, everyone, share, bool(backward)
             ),
             out_shape=jax.ShapeDtypeStruct(values.shape, BF16),
             scratch_shapes=[
-                pltpu.VMEM(pool, jnp.float32),
-                pltpu.VMEM((rows, kernels * lon_dev, 6 * LANES), BF16),
-                pltpu.VMEM((tables[backward].count(SMAX), kernels * lon_dev, 3 * LANES), BF16),
                 pltpu.VMEM((rows + 2, (2 * SMAX + 1) * lon_dev, height), BF16),
                 pltpu.VMEM((rows * lon_dev, kernels * height), BF16),
             ],
-            compiler_params=LARGE,
-        )(w_group, values, *filters, *halo)
-
-    mixed_in = exchange(convolve(columns, 0))
+            compiler_params=SMALL,
+        )(w_group, values, table, *halo)
+
+    mixed_in = convolve(columns, lay(filters, 0), 0)
+    mixed_in, filters = lax.optimization_barrier((mixed_in, filters))
+    mixed_in = exchange(mixed_in)
     outputs, grad_mixed = pl.pallas_call(
         dense_kernel,
         out_shape=(jax.ShapeDtypeStruct((cells, channels), BF16), square),
         compiler_params=SMALL,
     )(mixed_in.reshape(channels, cells), w_mix, grad_out.reshape(cells, channels))
-    grad_in = exchange(convolve(exchange(grad_mixed), 1))
+    grad_in = exchange(convolve(exchange(grad_mixed), lay(filters, 1), 1))
     grad_in = transposed(grad_in.reshape(channels, cells))
     return outputs.reshape(inputs.shape), grad_in.reshape(inputs.shape)
 

time: 54.1 us -> 57.5 us (1.063)
  blocking collectives: 29.7 us -> 20.4 us
  local copies, waits for them, and re-layouts: 0.02 us -> 7.22 us
  starting transfers between devices: 7.61 us -> 10.2 us
  Pallas kernels: 8.25 us -> 10.4 us
  waiting for transfers between devices: 7.58 us -> 8.16 us
    all_to_all x3 -> x2, blocking collectives: 29.7 us -> 20.4 us  [exchange(): return lax.all_to_all(parted, everyone, 0, 0)]
    unnamed x8 -> x18, local copies, waits for them, and re-layouts: 0.02 us -> 7.22 us
    all_to_all x1 -> x2, starting transfers between devices: 7.3 us -> 10 us  [exchange(): return lax.all_to_all(parted, everyone, 0, 0)]
    pallas_call x2 -> x4, Pallas kernels: 4.37 us -> 6.37 us  [the longest x2 4.16 us: convolve(): pl.pallas_call(partial(conv_kernel, wide[backward], rows, bands, lon_dev,...]
    all_to_all x1 -> x2, waiting for transfers between devices: 6.46 us -> 6.75 us  [exchange(): return lax.all_to_all(parted, everyone, 0, 0)]
  transfers between devices with their start and end apart: 2 -> 3, of which waited for: 2 -> 3; matrix products, arithmetic and copies ran while one was open for 0% -> 0% of each run, Pallas kernels for 0% -> 4%
where the time goes in v1:
time: 57.5 us; the launch traced here: 57.2 us
  blocking collectives  20.4 us (35%)
  Pallas kernels  10.4 us (18%)
  starting transfers between devices  10.2 us (18%)
  waiting for transfers between devices  8.16 us (14%)
  local copies, waits for them, and re-layouts  7.22 us (13%)
  between operations  0.72 us (1%)
    all_to_all x2, blocking collectives, exchange(): return lax.all_to_all(parted, everyone, 0, 0)  20.4 us
    all_to_all x2, starting transfers between devices, exchange(): return lax.all_to_all(parted, everyone, 0, 0)  10 us
    unnamed x18, local copies, waits for them, and re-layouts  7.22 us
    all_to_all x2, waiting for transfers between devices, exchange(): return lax.all_to_all(parted, everyone, 0, 0)  6.75 us
    pallas_call x2, Pallas kernels, convolve(): pl.pallas_call(partial(conv_kernel, wide[backward], rows, bands, lon_dev,...  4.16 us
    pallas_call x2, Pallas kernels, lay(): pl.pallas_call(partial(table_kernel, some, rows, bands, lon_dev, merged,...  2.2 us
    pallas_call x1, Pallas kernels, body(): pl.pallas_call(partial(enter_kernel, lon_dev), out_shape=(square, jax.Sha...  1.87 us
    ppermute x1, waiting for transfers between devices, body(): filters = [own_filters, lax.ppermute(own_filters, 'lat', [(0, 1), (1, 0)])]  1.4 us
  transfers between devices with their start and end apart: 3, of which 3 were waited for; matrix products, arithmetic and copies ran while one was open for 0% of the time, Pallas kernels for 4%

profile of v1, /device:TPU:0, one launch (start us, length us, event | category | flops | bytes accessed | tf_op | source)
XLA Modules:
  0.0 57.2 jit_solution(6872265972418180188)
XLA Ops:
  0.6 0.0 copy-start.8
  0.6 1.9 %shard_map.77 = (bf16[256,256]{1,0:T(8,128)(2,1)}, f32[4,3,8,384]{3,2,1,0:T(8,128)}) custom-call(s32[8]{0:T(128)} %w_ref.2, bf16[256,256]{1,0:T(8,128)(2,1)} %bitcast.20, f32[4,3,8,257]{3,2,1,0:T(8,128)} %bitcast.19), custom_call_target="tpu_custom_call" | custom-call | tf_op jit(solution)/shard_map/pallas_call | solution.py:281
  2.5 7.4 %all-to-all-start = ((bf16[32,8,256]{2,1,0:T(8,128)(2,1)}), bf16[32,8,256]{2,1,0:T(8,128)(2,1)}, u32[]{:S(2)}, u32[]{:S(2)}) async-start(bf16[32,8,256]{2,1,0:T(8,128)(2,1)} %bitcast.21), calls=%async_computation | async-start | bytes 262144 | tf_op jit(solution)/shard_map/all_to_all | solution.py:279
  9.9 0.2 collective-permute-start
  10.2 1.4 %collective-permute-done.refs_1_ = f32[4,3,8,384]{3,2,1,0:T(8,128)S(1)} collective-permute-done((f32[4,3,8,384]{3,2,1,0:T(8,128)}, f32[4,3,8,384]{3,2,1,0:T(8,128)S(1)}, u32[]{:S(2)}, u32[]{:S(2)}) %collective-permute-start) | collective-permute-done | bytes 147488 | tf_op jit(solution)/shard_map/ppermute | solution.py:295
  11.6 0.9 %copy-done.2 = f32[4,3,8,384]{3,2,1,0:T(8,128)S(1)} copy-done((f32[4,3,8,384]{3,2,1,0:T(8,128)S(1)}, f32[4,3,8,384]{3,2,1,0:T(8,128)}, u32[]{:S(2)}) %copy-start.2) | copy-done | bytes 147480
  12.5 1.0 %shard_map.78.refs_2_ = bf16[18,128,768]{2,1,0:T(8,128)(2,1)S(1)} custom-call(f32[4,3,8,384]{3,2,1,0:T(8,128)S(1)} %copy-done.2, f32[4,3,8,384]{3,2,1,0:T(8,128)S(1)} %collective-permute-done.refs_1_), custom_call_target="tpu_custom_call" | custom-call | tf_op jit(solution)/shard_map/pallas_call | solution.py:304
  13.5 0.0 copy-start.4
  13.5 0.6 %copy-done.4 = f32[4,3,8,384]{3,2,1,0:T(8,128)} copy-done((f32[4,3,8,384]{3,2,1,0:T(8,128)}, f32[4,3,8,384]{3,2,1,0:T(8,128)S(1)}, u32[]{:S(2)}) %copy-start.4) | copy-done | bytes 147480
  14.2 3.7 %all-to-all-done = bf16[32,8,256]{2,1,0:T(8,128)(2,1)} async-done(((bf16[32,8,256]{2,1,0:T(8,128)(2,1)}), bf16[32,8,256]{2,1,0:T(8,128)(2,1)}, u32[]{:S(2)}, u32[]{:S(2)}) %all-to-all-start) | async-done | bytes 131104 | tf_op jit(solution)/shard_map/all_to_all | solution.py:279
  17.8 0.0 copy-done.8
  17.8 2.6 %shard_map.79 = bf16[2,128,256]{2,1,0:T(8,128)(2,1)S(1)} custom-call(bf16[4,4,256]{2,1,0:T(4,128)(2,1)S(1)} %copy-done.8, bf16[2,128,256]{2,1,0:T(8,128)(2,1)} %bitcast.3.refs_1_, bf16[18,128,768]{2,1,0:T(8,128)(2,1)S(1)} %shard_map.78.refs_2_), custom_call_target="tpu_custom_call" | custom-call | tf_op jit(solution)/shard_map/pallas_call | solution.py:314
  20.4 9.9 %all_to_all.20 = bf16[32,8,256]{2,1,0:T(8,128)(2,1)S(1)} all-to-all(bf16[32,8,256]{2,1,0:T(8,128)(2,1)S(1)} %bitcast.17), channel_id=1, replica_groups=mesh['lon'=16,'lat'=2] {'lat','lon'}, dimensions={0} | all-to-all | bytes 262144 | tf_op jit(solution)/shard_map/all_to_all | solution.py:279
  30.4 1.3 %shard_map.80 = (bf16[256,256]{1,0:T(8,128)(2,1)}, bf16[256,256]{1,0:T(8,128)(2,1)}) custom-call(bf16[256,256]{1,0:T(8,128)(2,1)S(1)} %bitcast.14, bf16[256,256]{1,0:T(8,128)(2,1)S(1)} %copy-done.6, bf16[256,256]{1,0:T(8,128)(2,1)S(1)} %bitcast.18), custom_call_target="tpu_custom_call" | custom-call | tf_op jit(solution)/shard_map/pallas_call | solution.py:329
  31.7 2.6 %all-to-all-start.2 = ((bf16[32,8,256]{2,1,0:T(8,128)(2,1)}), bf16[32,8,256]{2,1,0:T(8,128)(2,1)S(1)}, u32[]{:S(2)}, u32[]{:S(2)}) async-start(bf16[32,8,256]{2,1,0:T(8,128)(2,1)} %bitcast.8), calls=%async_computation.2 | async-start | bytes 262144 | tf_op jit(solution)/shard_map/all_to_all | solution.py:279
  34.3 0.9 %copy-done.3 = f32[4,3,8,384]{3,2,1,0:T(8,128)S(1)} copy-done((f32[4,3,8,384]{3,2,1,0:T(8,128)S(1)}, f32[4,3,8,384]{3,2,1,0:T(8,128)}, u32[]{:S(2)}) %copy-start.3) | copy-done | bytes 147480
  35.2 0.9 %copy-done.5 = f32[4,3,8,384]{3,2,1,0:T(8,128)S(1)} copy-done((f32[4,3,8,384]{3,2,1,0:T(8,128)S(1)}, f32[4,3,8,384]{3,2,1,0:T(8,128)}, u32[]{:S(2)}) %copy-start.5) | copy-done | bytes 147480
  36.1 1.2 %shard_map.81.refs_2_ = bf16[19,128,768]{2,1,0:T(8,128)(2,1)S(1)} custom-call(f32[4,3,8,384]{3,2,1,0:T(8,128)S(1)} %copy-done.3, f32[4,3,8,384]{3,2,1,0:T(8,128)S(1)} %copy-done.5), custom_call_target="tpu_custom_call" | custom-call | tf_op jit(solution)/shard_map/pallas_call | solution.py:304
  37.3 1.8 %copy-done = bf16[19,128,768]{2,1,0:T(8,128)(2,1)} copy-done((bf16[19,128,768]{2,1,0:T(8,128)(2,1)}, bf16[19,128,768]{2,1,0:T(8,128)(2,1)S(1)}, u32[]{:S(2)}) %copy-start) | copy-done | bytes 3735576
  39.1 3.1 %all-to-all-done.2 = bf16[32,8,256]{2,1,0:T(8,128)(2,1)S(1)} async-done(((bf16[32,8,256]{2,1,0:T(8,128)(2,1)}), bf16[32,8,256]{2,1,0:T(8,128)(2,1)S(1)}, u32[]{:S(2)}, u32[]{:S(2)}) %all-to-all-start.2) | async-done | bytes 131104 | tf_op jit(solution)/shard_map/all_to_all | solution.py:279
  42.2 2.1 %copy-done.1 = bf16[19,128,768]{2,1,0:T(8,128)(2,1)S(1)} copy-done((bf16[19,128,768]{2,1,0:T(8,128)(2,1)S(1)}, bf16[19,128,768]{2,1,0:T(8,128)(2,1)}, u32[]{:S(2)}) %copy-start.1) | copy-done | bytes 3735576
  44.2 1.6 %shard_map.82 = bf16[2,128,256]{2,1,0:T(8,128)(2,1)S(1)} custom-call(bf16[4,4,256]{2,1,0:T(4,128)(2,1)S(1)} %copy-done.8, bf16[2,128,256]{2,1,0:T(8,128)(2,1)S(1)} %bitcast.13, bf16[19,128,768]{2,1,0:T(8,128)(2,1)S(1)} %copy-done.1), custom_call_target="tpu_custom_call" | custom-call | tf_op jit(solution)/shard_map/pallas_call | solution.py:314
  45.8 10.5 %all_to_all.21 = bf16[32,8,256]{2,1,0:T(8,128)(2,1)S(1)} all-to-all(bf16[32,8,256]{2,1,0:T(8,128)(2,1)S(1)} %bitcast.15), channel_id=1, replica_groups=mesh['lon'=16,'lat'=2] {'lat','lon'}, dimensions={0} | all-to-all | bytes 262144 | tf_op jit(solution)/shard_map/all_to_all | solution.py:279
  56.3 0.9 %shard_map.83 = bf16[256,256]{1,0:T(8,128)(2,1)} custom-call(bf16[256,256]{1,0:T(8,128)(2,1)S(1)} %bitcast.16), custom_call_target="tpu_custom_call" | custom-call | tf_op jit(solution)/shard_map/pallas_call | solution.py:47
  (9 shorter events, 0.0 us)
Async XLA Ops:
  0.6 17.2 %copy-start.8 = (bf16[4,4,256]{2,1,0:T(4,128)(2,1)S(1)}, bf16[4,4,256]{2,1,0:T(4,128)(2,1)}, u32[]{:S(2)}) copy-start(bf16[4,4,256]{2,1,0:T(4,128)(2,1)} %refs_0_.3) | copy-start | bytes 24580
  2.5 15.3 %all-to-all-start = ((bf16[32,8,256]{2,1,0:T(8,128)(2,1)}), bf16[32,8,256]{2,1,0:T(8,128)(2,1)}, u32[]{:S(2)}, u32[]{:S(2)}) async-start(bf16[32,8,256]{2,1,0:T(8,128)(2,1)} %bitcast.21), calls=%async_computation | async-start | bytes 262144 | tf_op jit(solution)/shard_map/all_to_all | solution.py:279
  9.9 1.6 %collective-permute-start = (f32[4,3,8,384]{3,2,1,0:T(8,128)}, f32[4,3,8,384]{3,2,1,0:T(8,128)S(1)}, u32[]{:S(2)}, u32[]{:S(2)}) collective-permute-start(f32[4,3,8,384]{3,2,1,0:T(8,128)} %get-tuple-element.14.refs_0_), channel_id=1, source_target_pairs={{0,1},{1,0},{2,3},{3,2},{4,5},{5,4},{6,7},{7,6},{8,9},{9,8},{10,11... | collective-permute-start | bytes 442376 | tf_op jit(solution)/shard_map/ppermute | solution.py:295
  11.6 0.9 %copy-start.2 = (f32[4,3,8,384]{3,2,1,0:T(8,128)S(1)}, f32[4,3,8,384]{3,2,1,0:T(8,128)}, u32[]{:S(2)}) copy-start(f32[4,3,8,384]{3,2,1,0:T(8,128)} %get-tuple-element.14.refs_0_) | copy-start | bytes 442372
  13.5 0.6 %copy-start.4 = (f32[4,3,8,384]{3,2,1,0:T(8,128)}, f32[4,3,8,384]{3,2,1,0:T(8,128)S(1)}, u32[]{:S(2)}) copy-start(f32[4,3,8,384]{3,2,1,0:T(8,128)S(1)} %collective-permute-done.refs_1_) | copy-start | bytes 442372
  17.8 12.5 %copy-start.6 = (bf16[256,256]{1,0:T(8,128)(2,1)S(1)}, bf16[256,256]{1,0:T(8,128)(2,1)}, u32[]{:S(2)}) copy-start(bf16[256,256]{1,0:T(8,128)(2,1)} %w_ref.3) | copy-start | bytes 393220
  17.8 12.5 %copy-start.7 = (bf16[8,32,256]{2,1,0:T(8,128)(2,1)S(1)}, bf16[8,32,256]{2,1,0:T(8,128)(2,1)}, u32[]{:S(2)}) copy-start(bf16[8,32,256]{2,1,0:T(8,128)(2,1)} %param.11) | copy-start | bytes 393220
  31.7 10.5 %all-to-all-start.2 = ((bf16[32,8,256]{2,1,0:T(8,128)(2,1)}), bf16[32,8,256]{2,1,0:T(8,128)(2,1)S(1)}, u32[]{:S(2)}, u32[]{:S(2)}) async-start(bf16[32,8,256]{2,1,0:T(8,128)(2,1)} %bitcast.8), calls=%async_computation.2 | async-start | bytes 262144 | tf_op jit(solution)/shard_map/all_to_all | solution.py:279
  34.3 0.9 %copy-start.3 = (f32[4,3,8,384]{3,2,1,0:T(8,128)S(1)}, f32[4,3,8,384]{3,2,1,0:T(8,128)}, u32[]{:S(2)}) copy-start(f32[4,3,8,384]{3,2,1,0:T(8,128)} %get-tuple-element.14.refs_0_) | copy-start | bytes 442372
  35.2 0.9 %copy-start.5 = (f32[4,3,8,384]{3,2,1,0:T(8,128)S(1)}, f32[4,3,8,384]{3,2,1,0:T(8,128)}, u32[]{:S(2)}) copy-start(f32[4,3,8,384]{3,2,1,0:T(8,128)} %copy-done.4) | copy-start | bytes 442372
  37.3 1.8 %copy-start = (bf16[19,128,768]{2,1,0:T(8,128)(2,1)}, bf16[19,128,768]{2,1,0:T(8,128)(2,1)S(1)}, u32[]{:S(2)}) copy-start(bf16[19,128,768]{2,1,0:T(8,128)(2,1)S(1)} %shard_map.81.refs_2_) | copy-start | bytes 11206660
  42.2 2.1 %copy-start.1 = (bf16[19,128,768]{2,1,0:T(8,128)(2,1)S(1)}, bf16[19,128,768]{2,1,0:T(8,128)(2,1)}, u32[]{:S(2)}) copy-start(bf16[19,128,768]{2,1,0:T(8,128)(2,1)} %copy-done) | copy-start | bytes 11206660

commit v2 on v0

--- a/solution.py
+++ b/solution.py
@@ -52,8 +52,14 @@
     )(values)
 
 
-def enter_kernel(lon_dev, w_ref, x_ref, p_ref, o_ref, f_ref):
+def enter_kernel(lon_dev, w_ref, x_hbm, p_hbm, o_ref, f_ref, x_ref, p_ref, x_done, p_done):
+    fetch_x = pltpu.make_async_copy(x_hbm, x_ref, x_done)
+    fetch_p = pltpu.make_async_copy(p_hbm, p_ref, p_done)
+    fetch_x.start()
+    fetch_p.start()
+    fetch_x.wait()
     o_ref[...] = turned_by_identity(x_ref[...])
+    fetch_p.wait()
     kernels, taps, rows, cells = p_ref.shape
     shape = (rows, LANES)
     line, lane = iota(shape, 0), iota(shape, 1)
@@ -178,12 +184,12 @@
     lay_toeplitz(rows, wide, lon_dev, merged, backward, f, t_ref, e_ref)
 
     def put(values, first):
-        values = values.T.astype(jnp.float32)
+        values = values.T
         count = values.shape[0] // lon_dev
         for shard in range(-SMAX, SMAX + 1):
             turned = pltpu.roll(values, -shard * share % height, 1) if shard else values
             at = pl.ds((shard + SMAX) * lon_dev, lon_dev)
-            xs[pl.ds(first + 1, count), at, :] = turned.astype(BF16).reshape(
+            xs[pl.ds(first + 1, count), at, :] = turned.reshape(
                 count, lon_dev, height
             )
 
@@ -279,9 +285,16 @@
         ),
         in_specs=[
             pl.BlockSpec(memory_space=pltpu.SMEM),
-            pl.BlockSpec(memory_space=pltpu.VMEM),
-            pl.BlockSpec(memory_space=pltpu.VMEM),
+            pl.BlockSpec(memory_space=pltpu.HBM),
+            pl.BlockSpec(memory_space=pltpu.HBM),
         ],
+        scratch_shapes=[
+            pltpu.VMEM((cells, channels), BF16),
+            pltpu.VMEM((kernels, 3, row_count, psi_raw.shape[-1]), jnp.float32),
+            pltpu.SemaphoreType.DMA,
+            pltpu.SemaphoreType.DMA,
+        ],
+        compiler_params=SMALL,
     )(widths, inputs.reshape(cells, channels), psi_raw.transpose(0, 2, 1, 3))
     columns = exchange(turned)
     if merged:

time: 54.1 us -> 56.4 us (1.043)
  local copies, waits for them, and re-layouts: 0.02 us -> 2.48 us
    unnamed x8 -> x12, local copies, waits for them, and re-layouts: 0.02 us -> 2.48 us
where the time goes in v2:
time: 56.4 us; the launch traced here: 56.1 us
  blocking collectives  29.7 us (53%)
  Pallas kernels  7.98 us (14%)
  starting transfers between devices  7.62 us (14%)
  waiting for transfers between devices  7.59 us (13%)
  local copies, waits for them, and re-layouts  2.48 us (4%)
  between operations  0.7 us (1%)
    all_to_all x3, blocking collectives, exchange(): return lax.all_to_all(parted, everyone, 0, 0)  29.7 us
    all_to_all x1, starting transfers between devices, exchange(): return lax.all_to_all(parted, everyone, 0, 0)  7.3 us
    all_to_all x1, waiting for transfers between devices, exchange(): return lax.all_to_all(parted, everyone, 0, 0)  6.47 us
    pallas_call x2, Pallas kernels, convolve(): pl.pallas_call(partial(conv_kernel, tables[backward], bands, lon_dev, mer...  4.16 us
    unnamed x12, local copies, waits for them, and re-layouts  2.48 us
    pallas_call x1, Pallas kernels, body(): pl.pallas_call(partial(enter_kernel, lon_dev), out_shape=(square, jax.Sha...  1.8 us
    pallas_call x1, Pallas kernels, body(): pl.pallas_call(dense_kernel, out_shape=(jax.ShapeDtypeStruct((cells, chan...  1.14 us
  transfers between devices with their start and end apart: 2, of which 2 were waited for; matrix products, arithmetic and copies ran while one was open for 0% of the time, Pallas kernels for 0%

profile of v2, /device:TPU:0, one launch (start us, length us, event | category | flops | bytes accessed | tf_op | source)
XLA Modules:
  0.0 56.1 jit_solution(17092492891589741842)
XLA Ops:
  0.6 0.0 copy-start.5
  0.6 0.6 %copy-done.5 = s32[8]{0:T(128)S(1)} copy-done((s32[8]{0:T(128)S(1)}, s32[8]{0:T(128)}, u32[]{:S(2)}) %copy-start.5) | copy-done | bytes 56
  1.3 0.0 copy-start
  1.3 0.9 %copy-done = f32[4,8,3,257]{3,1,2,0:T(8,128)S(1)} copy-done((f32[4,8,3,257]{3,1,2,0:T(8,128)S(1)}, f32[4,8,3,257]{3,1,2,0:T(8,128)}, u32[]{:S(2)}) %copy-start) | copy-done | bytes 98712
  2.2 0.0 copy-start.3
  2.2 0.9 %copy-done.3 = bf16[8,32,256]{2,1,0:T(8,128)(2,1)S(1)} copy-done((bf16[8,32,256]{2,1,0:T(8,128)(2,1)S(1)}, bf16[8,32,256]{2,1,0:T(8,128)(2,1)}, u32[]{:S(2)}) %copy-start.3) | copy-done | bytes 131096
  3.1 1.8 %shard_map.77 = (bf16[256,256]{1,0:T(8,128)(2,1)}, f32[4,3,8,384]{3,2,1,0:T(8,128)S(1)}) custom-call(s32[8]{0:T(128)S(1)} %copy-done.5, bf16[256,256]{1,0:T(8,128)(2,1)S(1)} %bitcast.21, f32[4,3,8,257]{3,2,1,0:T(8,128)S(1)} %bitcast.19), custom_call_target="tpu_custom_call" | custom-call | tf_op jit(solution)/shard_map/pallas_call | solution.py:280
  4.9 0.0 copy-start.4
  4.9 7.3 %all-to-all-start = ((bf16[32,8,256]{2,1,0:T(8,128)(2,1)}), bf16[32,8,256]{2,1,0:T(8,128)(2,1)S(1)}, u32[]{:S(2)}, u32[]{:S(2)}) async-start(bf16[32,8,256]{2,1,0:T(8,128)(2,1)} %bitcast.2), calls=%async_computation | async-start | bytes 262144 | tf_op jit(solution)/shard_map/all_to_all | solution.py:278
  12.2 0.3 collective-permute-start
  12.6 1.1 %collective-permute-done.refs_1_ = f32[4,3,8,384]{3,2,1,0:T(8,128)S(1)} collective-permute-done((f32[4,3,8,384]{3,2,1,0:T(8,128)S(1)}, f32[4,3,8,384]{3,2,1,0:T(8,128)S(1)}, u32[]{:S(2)}, u32[]{:S(2)}) %collective-permute-start) | collective-permute-done | bytes 147488 | tf_op jit(solution)/shard_map/ppermute | solution.py:301
  13.7 6.5 %all-to-all-done = bf16[32,8,256]{2,1,0:T(8,128)(2,1)S(1)} async-done(((bf16[32,8,256]{2,1,0:T(8,128)(2,1)}), bf16[32,8,256]{2,1,0:T(8,128)(2,1)S(1)}, u32[]{:S(2)}, u32[]{:S(2)}) %all-to-all-start) | async-done | bytes 131104 | tf_op jit(solution)/shard_map/all_to_all | solution.py:278
  20.1 0.0 copy-done.4
  20.1 2.0 %shard_map.78 = bf16[2,128,256]{2,1,0:T(8,128)(2,1)S(1)} custom-call(bf16[4,4,256]{2,1,0:T(4,128)(2,1)S(1)} %copy-done.4, bf16[2,128,256]{2,1,0:T(8,128)(2,1)S(1)} %bitcast.13, f32[4,3,8,384]{3,2,1,0:T(8,128)S(1)} %get-tuple-element.7.refs_0_, f32[4,3,8,384]{3,2,1,0:T(8,128)S(1)} %collective-permute-done.refs_1_), custom_call_target="tpu_custom_call" | custom-call | tf_op jit(solution)/shard_map/pallas_call | solution.py:310
  22.2 0.0 copy-start.1
  22.2 0.0 copy-start.2
  22.2 9.9 %all_to_all.20 = bf16[32,8,256]{2,1,0:T(8,128)(2,1)S(1)} all-to-all(bf16[32,8,256]{2,1,0:T(8,128)(2,1)S(1)} %bitcast.17), channel_id=1, replica_groups=mesh['lon'=16,'lat'=2] {'lat','lon'}, dimensions={0} | all-to-all | bytes 262144 | tf_op jit(solution)/shard_map/all_to_all | solution.py:278
  32.1 0.0 copy-done.1
  32.1 0.0 copy-done.2
  32.1 1.1 %shard_map.79 = (bf16[256,256]{1,0:T(8,128)(2,1)}, bf16[256,256]{1,0:T(8,128)(2,1)S(1)}) custom-call(bf16[256,256]{1,0:T(8,128)(2,1)S(1)} %bitcast.14, bf16[256,256]{1,0:T(8,128)(2,1)S(1)} %copy-done.1, bf16[256,256]{1,0:T(8,128)(2,1)S(1)} %bitcast.20), custom_call_target="tpu_custom_call" | custom-call | tf_op jit(solution)/shard_map/pallas_call | solution.py:327
  33.3 9.9 %all_to_all.21 = bf16[32,8,256]{2,1,0:T(8,128)(2,1)S(1)} all-to-all(bf16[32,8,256]{2,1,0:T(8,128)(2,1)S(1)} %bitcast.22), channel_id=1, replica_groups=mesh['lon'=16,'lat'=2] {'lat','lon'}, dimensions={0} | all-to-all | bytes 262144 | tf_op jit(solution)/shard_map/all_to_all | solution.py:278
  43.2 2.1 %shard_map.80 = bf16[2,128,256]{2,1,0:T(8,128)(2,1)S(1)} custom-call(bf16[4,4,256]{2,1,0:T(4,128)(2,1)S(1)} %copy-done.4, bf16[2,128,256]{2,1,0:T(8,128)(2,1)S(1)} %bitcast.15, f32[4,3,8,384]{3,2,1,0:T(8,128)S(1)} %get-tuple-element.7.refs_0_, f32[4,3,8,384]{3,2,1,0:T(8,128)S(1)} %collective-permute-done.refs_1_), custom_call_target="tpu_custom_call" | custom-call | tf_op jit(solution)/shard_map/pallas_call | solution.py:310
  45.3 9.9 %all_to_all.22 = bf16[32,8,256]{2,1,0:T(8,128)(2,1)S(1)} all-to-all(bf16[32,8,256]{2,1,0:T(8,128)(2,1)S(1)} %bitcast.16), channel_id=1, replica_groups=mesh['lon'=16,'lat'=2] {'lat','lon'}, dimensions={0} | all-to-all | bytes 262144 | tf_op jit(solution)/shard_map/all_to_all | solution.py:278
  55.2 0.9 %shard_map.81 = bf16[256,256]{1,0:T(8,128)(2,1)} custom-call(bf16[256,256]{1,0:T(8,128)(2,1)S(1)} %bitcast.18), custom_call_target="tpu_custom_call" | custom-call | tf_op jit(solution)/shard_map/pallas_call | solution.py:48
Async XLA Ops:
  0.6 0.7 %copy-start.5 = (s32[8]{0:T(128)S(1)}, s32[8]{0:T(128)}, u32[]{:S(2)}) copy-start(s32[8]{0:T(128)} %w_ref.4) | copy-start | bytes 100
  1.3 0.9 %copy-start = (f32[4,8,3,257]{3,1,2,0:T(8,128)S(1)}, f32[4,8,3,257]{3,1,2,0:T(8,128)}, u32[]{:S(2)}) copy-start(f32[4,8,3,257]{3,1,2,0:T(8,128)} %param.7) | copy-start | bytes 296068
  2.2 0.9 %copy-start.3 = (bf16[8,32,256]{2,1,0:T(8,128)(2,1)S(1)}, bf16[8,32,256]{2,1,0:T(8,128)(2,1)}, u32[]{:S(2)}) copy-start(bf16[8,32,256]{2,1,0:T(8,128)(2,1)} %param.6) | copy-start | bytes 393220
  4.9 15.2 %copy-start.4 = (bf16[4,4,256]{2,1,0:T(4,128)(2,1)S(1)}, bf16[4,4,256]{2,1,0:T(4,128)(2,1)}, u32[]{:S(2)}) copy-start(bf16[4,4,256]{2,1,0:T(4,128)(2,1)} %w_ref.7) | copy-start | bytes 24580
  4.9 15.2 %all-to-all-start = ((bf16[32,8,256]{2,1,0:T(8,128)(2,1)}), bf16[32,8,256]{2,1,0:T(8,128)(2,1)S(1)}, u32[]{:S(2)}, u32[]{:S(2)}) async-start(bf16[32,8,256]{2,1,0:T(8,128)(2,1)} %bitcast.2), calls=%async_computation | async-start | bytes 262144 | tf_op jit(solution)/shard_map/all_to_all | solution.py:278
  12.2 1.4 %collective-permute-start = (f32[4,3,8,384]{3,2,1,0:T(8,128)S(1)}, f32[4,3,8,384]{3,2,1,0:T(8,128)S(1)}, u32[]{:S(2)}, u32[]{:S(2)}) collective-permute-start(f32[4,3,8,384]{3,2,1,0:T(8,128)S(1)} %get-tuple-element.7.refs_0_), channel_id=1, source_target_pairs={{0,1},{1,0},{2,3},{3,2},{4,5},{5,4},{6,7},{7,6},{8,9},{9,8},{10,11... | collective-permute-start | bytes 442376 | tf_op jit(solution)/shard_map/ppermute | solution.py:301
  22.2 9.9 %copy-start.1 = (bf16[256,256]{1,0:T(8,128)(2,1)S(1)}, bf16[256,256]{1,0:T(8,128)(2,1)}, u32[]{:S(2)}) copy-start(bf16[256,256]{1,0:T(8,128)(2,1)} %w_ref.6) | copy-start | bytes 393220
  22.2 9.9 %copy-start.2 = (bf16[8,32,256]{2,1,0:T(8,128)(2,1)S(1)}, bf16[8,32,256]{2,1,0:T(8,128)(2,1)}, u32[]{:S(2)}) copy-start(bf16[8,32,256]{2,1,0:T(8,128)(2,1)} %param.11) | copy-start | bytes 393220

commit v3 on v0

--- a/solution.py
+++ b/solution.py
@@ -52,8 +52,19 @@
     )(values)
 
 
-def enter_kernel(lon_dev, w_ref, x_ref, p_ref, o_ref, f_ref):
+def enter_kernel(
+    lon_dev, w_ref, x_far, p_far, o_far, f_far, x_ref, p_ref, o_ref, f_ref, done
+):
+    fetch_x = pltpu.make_async_copy(x_far, x_ref, done.at[0])
+    fetch_p = pltpu.make_async_copy(p_far, p_ref, done.at[1])
+    store_o = pltpu.make_async_copy(o_ref, o_far, done.at[2])
+    store_f = pltpu.make_async_copy(f_ref, f_far, done.at[3])
+    fetch_x.start()
+    fetch_p.start()
+    fetch_x.wait()
     o_ref[...] = turned_by_identity(x_ref[...])
+    store_o.start()
+    fetch_p.wait()
     kernels, taps, rows, cells = p_ref.shape
     shape = (rows, LANES)
     line, lane = iota(shape, 0), iota(shape, 1)
@@ -74,6 +85,9 @@
                 f_ref[k, tap, :, pl.ds(tile * LANES, LANES)] = (
                     (values * keep).astype(BF16).astype(jnp.float32)
                 )
+    store_f.start()
+    store_o.wait()
+    store_f.wait()
 
 
 def collect(bands, merged, backward, filter_refs, f):
@@ -178,12 +192,12 @@
     lay_toeplitz(rows, wide, lon_dev, merged, backward, f, t_ref, e_ref)
 
     def put(values, first):
-        values = values.T.astype(jnp.float32)
+        values = values.T
         count = values.shape[0] // lon_dev
         for shard in range(-SMAX, SMAX + 1):
             turned = pltpu.roll(values, -shard * share % height, 1) if shard else values
             at = pl.ds((shard + SMAX) * lon_dev, lon_dev)
-            xs[pl.ds(first + 1, count), at, :] = turned.astype(BF16).reshape(
+            xs[pl.ds(first + 1, count), at, :] = turned.reshape(
                 count, lon_dev, height
             )
 
@@ -271,17 +285,21 @@
         parted = values.reshape(segments * blocks, share, cells)
         return lax.all_to_all(parted, everyone, 0, 0)
 
+    shapes = [
+        (cells, channels),
+        (kernels, 3, row_count, psi_raw.shape[-1]),
+        (channels, cells),
+        (kernels, 3, row_count, 3 * LANES),
+    ]
+    kinds = [BF16, jnp.float32, BF16, jnp.float32]
+    anywhere = pl.BlockSpec(memory_space=pl.ANY)
     turned, own_filters = pl.pallas_call(
         partial(enter_kernel, lon_dev),
-        out_shape=(
-            square,
-            jax.ShapeDtypeStruct((kernels, 3, row_count, 3 * LANES), jnp.float32),
-        ),
-        in_specs=[
-            pl.BlockSpec(memory_space=pltpu.SMEM),
-            pl.BlockSpec(memory_space=pltpu.VMEM),
-            pl.BlockSpec(memory_space=pltpu.VMEM),
-        ],
+        out_shape=[jax.ShapeDtypeStruct(*some) for some in list(zip(shapes, kinds))[2:]],
+        in_specs=[pl.BlockSpec(memory_space=pltpu.SMEM), anywhere, anywhere],
+        out_specs=[anywhere, anywhere],
+        scratch_shapes=[pltpu.VMEM(*some) for some in zip(shapes, kinds)]
+        + [pltpu.SemaphoreType.DMA((4,))],
     )(widths, inputs.reshape(cells, channels), psi_raw.transpose(0, 2, 1, 3))
     columns = exchange(turned)
     if merged:

time: 54.1 us -> 54.7 us (1.011)
    pallas_call x1, Pallas kernels: 1.87 us -> 2.56 us  [body(): pl.pallas_call(partial(enter_kernel, lon_dev), out_shape=[jax.ShapeDtypeS...]
where the time goes in v3:
time: 54.7 us; the launch traced here: 54.4 us
  blocking collectives  29.7 us (54%)
  Pallas kernels  8.75 us (16%)
  starting transfers between devices  7.62 us (14%)
  waiting for transfers between devices  7.58 us (14%)
  between operations  0.71 us (1%)
    all_to_all x3, blocking collectives, exchange(): return lax.all_to_all(parted, everyone, 0, 0)  29.7 us
    all_to_all x1, starting transfers between devices, exchange(): return lax.all_to_all(parted, everyone, 0, 0)  7.3 us
    all_to_all x1, waiting for transfers between devices, exchange(): return lax.all_to_all(parted, everyone, 0, 0)  6.46 us
    pallas_call x2, Pallas kernels, convolve(): pl.pallas_call(partial(conv_kernel, tables[backward], bands, lon_dev, mer...  4.17 us
    pallas_call x1, Pallas kernels, body(): pl.pallas_call(partial(enter_kernel, lon_dev), out_shape=[jax.ShapeDtypeS...  2.56 us
    pallas_call x1, Pallas kernels, body(): pl.pallas_call(dense_kernel, out_shape=(jax.ShapeDtypeStruct((cells, chan...  1.14 us
    ppermute x1, waiting for transfers between devices, body(): filters = [own_filters, lax.ppermute(own_filters, 'lat', [(0, 1), (1, 0)])]  1.12 us
  transfers between devices with their start and end apart: 2, of which 2 were waited for; matrix products, arithmetic and copies ran while one was open for 0% of the time, Pallas kernels for 0%

profile of v3, /device:TPU:0, one launch (start us, length us, event | category | flops | bytes accessed | tf_op | source)
XLA Modules:
  0.0 54.4 jit_solution(8632318730856492348)
XLA Ops:
  0.6 2.6 %shard_map.77 = (bf16[256,256]{1,0:T(8,128)(2,1)}, f32[4,3,8,384]{3,2,1,0:T(8,128)}) custom-call(s32[8]{0:T(128)} %w_ref.4, bf16[256,256]{1,0:T(8,128)(2,1)} %bitcast.22, f32[4,3,8,257]{3,2,1,0:T(8,128)} %bitcast.21), custom_call_target="tpu_custom_call" | custom-call | tf_op jit(solution)/shard_map/pallas_call | solution.py:296
  3.2 0.0 copy-start
  3.2 0.0 copy-start.3
  3.2 7.3 %all-to-all-start = ((bf16[32,8,256]{2,1,0:T(8,128)(2,1)}), bf16[32,8,256]{2,1,0:T(8,128)(2,1)S(1)}, u32[]{:S(2)}, u32[]{:S(2)}) async-start(bf16[32,8,256]{2,1,0:T(8,128)(2,1)} %bitcast.23), calls=%async_computation | async-start | bytes 262144 | tf_op jit(solution)/shard_map/all_to_all | solution.py:286
  10.5 0.0 copy-done
  10.5 0.3 collective-permute-start
  10.9 1.1 %collective-permute-done.refs_1_ = f32[4,3,8,384]{3,2,1,0:T(8,128)S(1)} collective-permute-done((f32[4,3,8,384]{3,2,1,0:T(8,128)S(1)}, f32[4,3,8,384]{3,2,1,0:T(8,128)S(1)}, u32[]{:S(2)}, u32[]{:S(2)}) %collective-permute-start) | collective-permute-done | bytes 147488 | tf_op jit(solution)/shard_map/ppermute | solution.py:306
  12.0 6.5 %all-to-all-done = bf16[32,8,256]{2,1,0:T(8,128)(2,1)S(1)} async-done(((bf16[32,8,256]{2,1,0:T(8,128)(2,1)}), bf16[32,8,256]{2,1,0:T(8,128)(2,1)S(1)}, u32[]{:S(2)}, u32[]{:S(2)}) %all-to-all-start) | async-done | bytes 131104 | tf_op jit(solution)/shard_map/all_to_all | solution.py:286
  18.4 0.0 copy-done.3
  18.4 2.0 %shard_map.78 = bf16[2,128,256]{2,1,0:T(8,128)(2,1)S(1)} custom-call(bf16[4,4,256]{2,1,0:T(4,128)(2,1)S(1)} %copy-done.3, bf16[2,128,256]{2,1,0:T(8,128)(2,1)S(1)} %bitcast.13, f32[4,3,8,384]{3,2,1,0:T(8,128)S(1)} %copy-done, f32[4,3,8,384]{3,2,1,0:T(8,128)S(1)} %collective-permute-done.refs_1_), custom_call_target="tpu_custom_call" | custom-call | tf_op jit(solution)/shard_map/pallas_call | solution.py:315
  20.5 0.0 copy-start.1
  20.5 0.0 copy-start.2
  20.5 9.9 %all_to_all.20 = bf16[32,8,256]{2,1,0:T(8,128)(2,1)S(1)} all-to-all(bf16[32,8,256]{2,1,0:T(8,128)(2,1)S(1)} %bitcast.17), channel_id=1, replica_groups=mesh['lon'=16,'lat'=2] {'lat','lon'}, dimensions={0} | all-to-all | bytes 262144 | tf_op jit(solution)/shard_map/all_to_all | solution.py:286
  30.4 0.0 copy-done.1
  30.4 0.0 copy-done.2
  30.4 1.1 %shard_map.79 = (bf16[256,256]{1,0:T(8,128)(2,1)}, bf16[256,256]{1,0:T(8,128)(2,1)S(1)}) custom-call(bf16[256,256]{1,0:T(8,128)(2,1)S(1)} %bitcast.14, bf16[256,256]{1,0:T(8,128)(2,1)S(1)} %copy-done.1, bf16[256,256]{1,0:T(8,128)(2,1)S(1)} %bitcast.19), custom_call_target="tpu_custom_call" | custom-call | tf_op jit(solution)/shard_map/pallas_call | solution.py:332
  31.6 9.9 %all_to_all.21 = bf16[32,8,256]{2,1,0:T(8,128)(2,1)S(1)} all-to-all(bf16[32,8,256]{2,1,0:T(8,128)(2,1)S(1)} %bitcast.20), channel_id=1, replica_groups=mesh['lon'=16,'lat'=2] {'lat','lon'}, dimensions={0} | all-to-all | bytes 262144 | tf_op jit(solution)/shard_map/all_to_all | solution.py:286
  41.5 2.1 %shard_map.80 = bf16[2,128,256]{2,1,0:T(8,128)(2,1)S(1)} custom-call(bf16[4,4,256]{2,1,0:T(4,128)(2,1)S(1)} %copy-done.3, bf16[2,128,256]{2,1,0:T(8,128)(2,1)S(1)} %bitcast.15, f32[4,3,8,384]{3,2,1,0:T(8,128)S(1)} %copy-done, f32[4,3,8,384]{3,2,1,0:T(8,128)S(1)} %collective-permute-done.refs_1_), custom_call_target="tpu_custom_call" | custom-call | tf_op jit(solution)/shard_map/pallas_call | solution.py:315
  43.6 9.9 %all_to_all.22 = bf16[32,8,256]{2,1,0:T(8,128)(2,1)S(1)} all-to-all(bf16[32,8,256]{2,1,0:T(8,128)(2,1)S(1)} %bitcast.16), channel_id=1, replica_groups=mesh['lon'=16,'lat'=2] {'lat','lon'}, dimensions={0} | all-to-all | bytes 262144 | tf_op jit(solution)/shard_map/all_to_all | solution.py:286
  53.5 0.9 %shard_map.81 = bf16[256,256]{1,0:T(8,128)(2,1)} custom-call(bf16[256,256]{1,0:T(8,128)(2,1)S(1)} %bitcast.18), custom_call_target="tpu_custom_call" | custom-call | tf_op jit(solution)/shard_map/pallas_call | solution.py:48
Async XLA Ops:
  3.2 7.3 %copy-start = (f32[4,3,8,384]{3,2,1,0:T(8,128)S(1)}, f32[4,3,8,384]{3,2,1,0:T(8,128)}, u32[]{:S(2)}) copy-start(f32[4,3,8,384]{3,2,1,0:T(8,128)} %get-tuple-element.7.refs_0_) | copy-start | bytes 442372
  3.2 15.2 %copy-start.3 = (bf16[4,4,256]{2,1,0:T(4,128)(2,1)S(1)}, bf16[4,4,256]{2,1,0:T(4,128)(2,1)}, u32[]{:S(2)}) copy-start(bf16[4,4,256]{2,1,0:T(4,128)(2,1)} %w_ref.7) | copy-start | bytes 24580
  3.2 15.2 %all-to-all-start = ((bf16[32,8,256]{2,1,0:T(8,128)(2,1)}), bf16[32,8,256]{2,1,0:T(8,128)(2,1)S(1)}, u32[]{:S(2)}, u32[]{:S(2)}) async-start(bf16[32,8,256]{2,1,0:T(8,128)(2,1)} %bitcast.23), calls=%async_computation | async-start | bytes 262144 | tf_op jit(solution)/shard_map/all_to_all | solution.py:286
  10.5 1.4 %collective-permute-start = (f32[4,3,8,384]{3,2,1,0:T(8,128)S(1)}, f32[4,3,8,384]{3,2,1,0:T(8,128)S(1)}, u32[]{:S(2)}, u32[]{:S(2)}) collective-permute-start(f32[4,3,8,384]{3,2,1,0:T(8,128)S(1)} %copy-done), channel_id=1, source_target_pairs={{0,1},{1,0},{2,3},{3,2},{4,5},{5,4},{6,7},{7,6},{8,9},{9,8},{10,11... | collective-permute-start | bytes 442376 | tf_op jit(solution)/shard_map/ppermute | solution.py:306
  20.5 9.9 %copy-start.1 = (bf16[256,256]{1,0:T(8,128)(2,1)S(1)}, bf16[256,256]{1,0:T(8,128)(2,1)}, u32[]{:S(2)}) copy-start(bf16[256,256]{1,0:T(8,128)(2,1)} %w_ref.6) | copy-start | bytes 393220
  20.5 9.9 %copy-start.2 = (bf16[8,32,256]{2,1,0:T(8,128)(2,1)S(1)}, bf16[8,32,256]{2,1,0:T(8,128)(2,1)}, u32[]{:S(2)}) copy-start(bf16[8,32,256]{2,1,0:T(8,128)(2,1)} %param.11) | copy-start | bytes 393220

commit v4 on v0

--- a/solution.py
+++ b/solution.py
@@ -34,14 +34,8 @@
     return lax.broadcasted_iota(jnp.int32, shape, axis)
 
 
-def turned_by_identity(values):
-    count = values.shape[1]
-    unit = jnp.where(iota((count, count), 0) == iota((count, count), 1), 1.0, 0.0).astype(BF16)
-    return lax.dot_general(unit, values, ALONG, preferred_element_type=jnp.float32).astype(BF16)
-
-
 def transpose_kernel(x_ref, o_ref):
-    o_ref[...] = turned_by_identity(x_ref[...])
+    o_ref[...] = x_ref[...].T
 
 
 def transposed(values):
@@ -53,7 +47,7 @@
 
 
 def enter_kernel(lon_dev, w_ref, x_ref, p_ref, o_ref, f_ref):
-    o_ref[...] = turned_by_identity(x_ref[...])
+    o_ref[...] = x_ref[...].T
     kernels, taps, rows, cells = p_ref.shape
     shape = (rows, LANES)
     line, lane = iota(shape, 0), iota(shape, 1)
@@ -178,12 +172,12 @@
     lay_toeplitz(rows, wide, lon_dev, merged, backward, f, t_ref, e_ref)
 
     def put(values, first):
-        values = values.T.astype(jnp.float32)
+        values = values.T
         count = values.shape[0] // lon_dev
         for shard in range(-SMAX, SMAX + 1):
             turned = pltpu.roll(values, -shard * share % height, 1) if shard else values
             at = pl.ds((shard + SMAX) * lon_dev, lon_dev)
-            xs[pl.ds(first + 1, count), at, :] = turned.astype(BF16).reshape(
+            xs[pl.ds(first + 1, count), at, :] = turned.reshape(
                 count, lon_dev, height
             )
 
@@ -229,8 +223,8 @@
 
 
 def dense_kernel(m_ref, w_ref, g_ref, o_ref, d_ref):
-    mixed_in = turned_by_identity(m_ref[...])
-    pre = jnp.dot(mixed_in, w_ref[...], preferred_element_type=jnp.float32)
+    across = (((0,), (0,)), ((), ()))
+    pre = lax.dot_general(m_ref[...], w_ref[...], across, preferred_element_type=jnp.float32)
     slope = 0.7978845608028654
     square = pre * pre
     bent = jnp.tanh(slope * (pre + 0.044715 * (square * pre)))

time: 54.1 us -> 53.6 us (level)
  no operation moved by 1% of the time
where the time goes in v4:
time: 53.6 us; the launch traced here: 53.4 us
  blocking collectives  29.7 us (55%)
  Pallas kernels  7.72 us (14%)
  starting transfers between devices  7.61 us (14%)
  waiting for transfers between devices  7.58 us (14%)
  between operations  0.68 us (1%)
    all_to_all x3, blocking collectives, exchange(): return lax.all_to_all(parted, everyone, 0, 0)  29.7 us
    all_to_all x1, starting transfers between devices, exchange(): return lax.all_to_all(parted, everyone, 0, 0)  7.3 us
    all_to_all x1, waiting for transfers between devices, exchange(): return lax.all_to_all(parted, everyone, 0, 0)  6.46 us
    pallas_call x2, Pallas kernels, convolve(): pl.pallas_call(partial(conv_kernel, tables[backward], bands, lon_dev, mer...  4.17 us
    pallas_call x1, Pallas kernels, body(): pl.pallas_call(partial(enter_kernel, lon_dev), out_shape=(square, jax.Sha...  1.8 us
    ppermute x1, waiting for transfers between devices, body(): filters = [own_filters, lax.ppermute(own_filters, 'lat', [(0, 1), (1, 0)])]  1.12 us
  transfers between devices with their start and end apart: 2, of which 2 were waited for; matrix products, arithmetic and copies ran while one was open for 0% of the time, Pallas kernels for 0%

profile of v4, /device:TPU:0, one launch (start us, length us, event | category | flops | bytes accessed | tf_op | source)
XLA Modules:
  0.0 53.4 jit_solution(1815419503909537331)
XLA Ops:
  0.6 1.8 %shard_map.77 = (bf16[256,256]{1,0:T(8,128)(2,1)}, f32[4,3,8,384]{3,2,1,0:T(8,128)}) custom-call(s32[8]{0:T(128)} %w_ref.4, bf16[256,256]{1,0:T(8,128)(2,1)} %bitcast.22, f32[4,3,8,257]{3,2,1,0:T(8,128)} %bitcast.21), custom_call_target="tpu_custom_call" | custom-call | tf_op jit(solution)/shard_map/pallas_call | solution.py:268
  2.4 0.0 copy-start
  2.4 0.0 copy-start.3
  2.4 7.3 %all-to-all-start = ((bf16[32,8,256]{2,1,0:T(8,128)(2,1)}), bf16[32,8,256]{2,1,0:T(8,128)(2,1)S(1)}, u32[]{:S(2)}, u32[]{:S(2)}) async-start(bf16[32,8,256]{2,1,0:T(8,128)(2,1)} %bitcast.23), calls=%async_computation | async-start | bytes 262144 | tf_op jit(solution)/shard_map/all_to_all | solution.py:266
  9.7 0.0 copy-done
  9.7 0.3 collective-permute-start
  10.1 1.1 %collective-permute-done.refs_1_ = f32[4,3,8,384]{3,2,1,0:T(8,128)S(1)} collective-permute-done((f32[4,3,8,384]{3,2,1,0:T(8,128)S(1)}, f32[4,3,8,384]{3,2,1,0:T(8,128)S(1)}, u32[]{:S(2)}, u32[]{:S(2)}) %collective-permute-start) | collective-permute-done | bytes 147488 | tf_op jit(solution)/shard_map/ppermute | solution.py:282
  11.2 6.5 %all-to-all-done = bf16[32,8,256]{2,1,0:T(8,128)(2,1)S(1)} async-done(((bf16[32,8,256]{2,1,0:T(8,128)(2,1)}), bf16[32,8,256]{2,1,0:T(8,128)(2,1)S(1)}, u32[]{:S(2)}, u32[]{:S(2)}) %all-to-all-start) | async-done | bytes 131104 | tf_op jit(solution)/shard_map/all_to_all | solution.py:266
  17.6 0.0 copy-done.3
  17.7 2.0 %shard_map.78 = bf16[2,128,256]{2,1,0:T(8,128)(2,1)S(1)} custom-call(bf16[4,4,256]{2,1,0:T(4,128)(2,1)S(1)} %copy-done.3, bf16[2,128,256]{2,1,0:T(8,128)(2,1)S(1)} %bitcast.13, f32[4,3,8,384]{3,2,1,0:T(8,128)S(1)} %copy-done, f32[4,3,8,384]{3,2,1,0:T(8,128)S(1)} %collective-permute-done.refs_1_), custom_call_target="tpu_custom_call" | custom-call | tf_op jit(solution)/shard_map/pallas_call | solution.py:291
  19.7 0.0 copy-start.1
  19.7 0.0 copy-start.2
  19.7 9.9 %all_to_all.20 = bf16[32,8,256]{2,1,0:T(8,128)(2,1)S(1)} all-to-all(bf16[32,8,256]{2,1,0:T(8,128)(2,1)S(1)} %bitcast.17), channel_id=1, replica_groups=mesh['lon'=16,'lat'=2] {'lat','lon'}, dimensions={0} | all-to-all | bytes 262144 | tf_op jit(solution)/shard_map/all_to_all | solution.py:266
  29.6 0.0 copy-done.1
  29.6 0.0 copy-done.2
  29.6 1.0 %shard_map.79 = (bf16[256,256]{1,0:T(8,128)(2,1)}, bf16[256,256]{1,0:T(8,128)(2,1)S(1)}) custom-call(bf16[256,256]{1,0:T(8,128)(2,1)S(1)} %bitcast.14, bf16[256,256]{1,0:T(8,128)(2,1)S(1)} %copy-done.1, bf16[256,256]{1,0:T(8,128)(2,1)S(1)} %bitcast.19), custom_call_target="tpu_custom_call" | custom-call | tf_op jit(solution)/shard_map/pallas_call | solution.py:308
  30.6 9.9 %all_to_all.21 = bf16[32,8,256]{2,1,0:T(8,128)(2,1)S(1)} all-to-all(bf16[32,8,256]{2,1,0:T(8,128)(2,1)S(1)} %bitcast.20), channel_id=1, replica_groups=mesh['lon'=16,'lat'=2] {'lat','lon'}, dimensions={0} | all-to-all | bytes 262144 | tf_op jit(solution)/shard_map/all_to_all | solution.py:266
  40.5 2.1 %shard_map.80 = bf16[2,128,256]{2,1,0:T(8,128)(2,1)S(1)} custom-call(bf16[4,4,256]{2,1,0:T(4,128)(2,1)S(1)} %copy-done.3, bf16[2,128,256]{2,1,0:T(8,128)(2,1)S(1)} %bitcast.15, f32[4,3,8,384]{3,2,1,0:T(8,128)S(1)} %copy-done, f32[4,3,8,384]{3,2,1,0:T(8,128)S(1)} %collective-permute-done.refs_1_), custom_call_target="tpu_custom_call" | custom-call | tf_op jit(solution)/shard_map/pallas_call | solution.py:291
  42.7 9.9 %all_to_all.22 = bf16[32,8,256]{2,1,0:T(8,128)(2,1)S(1)} all-to-all(bf16[32,8,256]{2,1,0:T(8,128)(2,1)S(1)} %bitcast.16), channel_id=1, replica_groups=mesh['lon'=16,'lat'=2] {'lat','lon'}, dimensions={0} | all-to-all | bytes 262144 | tf_op jit(solution)/shard_map/all_to_all | solution.py:266
  52.6 0.7 %shard_map.81 = bf16[256,256]{1,0:T(8,128)(2,1)} custom-call(bf16[256,256]{1,0:T(8,128)(2,1)S(1)} %bitcast.18), custom_call_target="tpu_custom_call" | custom-call | tf_op jit(solution)/shard_map/pallas_call | solution.py:42
Async XLA Ops:
  2.4 7.3 %copy-start = (f32[4,3,8,384]{3,2,1,0:T(8,128)S(1)}, f32[4,3,8,384]{3,2,1,0:T(8,128)}, u32[]{:S(2)}) copy-start(f32[4,3,8,384]{3,2,1,0:T(8,128)} %get-tuple-element.7.refs_0_) | copy-start | bytes 442372
  2.4 15.2 %copy-start.3 = (bf16[4,4,256]{2,1,0:T(4,128)(2,1)S(1)}, bf16[4,4,256]{2,1,0:T(4,128)(2,1)}, u32[]{:S(2)}) copy-start(bf16[4,4,256]{2,1,0:T(4,128)(2,1)} %w_ref.7) | copy-start | bytes 24580
  2.4 15.2 %all-to-all-start = ((bf16[32,8,256]{2,1,0:T(8,128)(2,1)}), bf16[32,8,256]{2,1,0:T(8,128)(2,1)S(1)}, u32[]{:S(2)}, u32[]{:S(2)}) async-start(bf16[32,8,256]{2,1,0:T(8,128)(2,1)} %bitcast.23), calls=%async_computation | async-start | bytes 262144 | tf_op jit(solution)/shard_map/all_to_all | solution.py:266
  9.7 1.4 %collective-permute-start = (f32[4,3,8,384]{3,2,1,0:T(8,128)S(1)}, f32[4,3,8,384]{3,2,1,0:T(8,128)S(1)}, u32[]{:S(2)}, u32[]{:S(2)}) collective-permute-start(f32[4,3,8,384]{3,2,1,0:T(8,128)S(1)} %copy-done), channel_id=1, source_target_pairs={{0,1},{1,0},{2,3},{3,2},{4,5},{5,4},{6,7},{7,6},{8,9},{9,8},{10,11... | collective-permute-start | bytes 442376 | tf_op jit(solution)/shard_map/ppermute | solution.py:282
  19.7 9.9 %copy-start.1 = (bf16[256,256]{1,0:T(8,128)(2,1)S(1)}, bf16[256,256]{1,0:T(8,128)(2,1)}, u32[]{:S(2)}) copy-start(bf16[256,256]{1,0:T(8,128)(2,1)} %w_ref.6) | copy-start | bytes 393220
  19.7 9.9 %copy-start.2 = (bf16[8,32,256]{2,1,0:T(8,128)(2,1)S(1)}, bf16[8,32,256]{2,1,0:T(8,128)(2,1)}, u32[]{:S(2)}) copy-start(bf16[8,32,256]{2,1,0:T(8,128)(2,1)} %param.11) | copy-start | bytes 393220

commit v5 on v4

--- a/solution.py
+++ b/solution.py
@@ -88,13 +88,13 @@
             f[segment] = values.reshape(kernels, taps, lines, width)
 
 
-def lay_toeplitz(rows, wide, lon_dev, merged, backward, f, t_ref, e_ref):
+def lay_toeplitz(rows, wide, lon_dev, merged, backward, f, t_ref, e_ref=None):
     segments, kernels, _, held, _ = f.shape
     shape = (lon_dev, LANES)
     lane, line = iota(shape, 1), iota(shape, 0)
     upper = lane >= line
     corner = lane == line
-    for row in range(rows):
+    for place, row in enumerate(rows):
         for tap in range(3):
             source, column = (row + tap - 1, 2 - tap) if backward else (row, tap)
             source += 0 if merged else held
@@ -114,8 +114,8 @@
                 else:
                     parts = [jnp.zeros(shape, jnp.float32)] * 2
                 for i, part in enumerate(parts):
-                    t_ref[row, here, pl.ds((tap * 2 + i) * LANES, LANES)] = part.astype(BF16)
-                if row in wide:
+                    t_ref[place, here, pl.ds((tap * 2 + i) * LANES, LANES)] = part.astype(BF16)
+                if e_ref is not None and row in wide:
                     last = parts[0]
                     if present:
                         last = jnp.where(corner, turned(2), jnp.where(upper, 0.0, second))
@@ -157,8 +157,19 @@
     return jnp.where(same, spread, 0.0).astype(BF16)
 
 
+def rows_ahead(rows, wide):
+    ahead = [row for row in range(rows // 4, rows - rows // 4) if row not in wide]
+    return ahead, [row for row in range(rows) if row not in ahead]
+
+
+def table_kernel(wide, rows, bands, lon_dev, merged, backward, *refs):
+    *filter_refs, t_ref, f = refs
+    collect(bands, merged, backward, filter_refs, f)
+    lay_toeplitz(rows_ahead(rows, wide)[0], wide, lon_dev, merged, backward, f, t_ref)
+
+
 def conv_kernel(
-    table, bands, lon_dev, merged, everyone, share, backward, w_ref, own_ref, *refs
+    table, bands, lon_dev, merged, everyone, share, backward, w_ref, own_ref, ahead_ref, *refs
 ):
     count = 2 if merged else 3
     filter_refs, refs = refs[:count], refs[count:]
@@ -168,8 +179,9 @@
     held = rows // segments
     kernels = f.shape[1]
     wide = [row for row, reach in enumerate(table) if reach == SMAX]
+    ahead, others = rows_ahead(rows, wide)
     collect(bands, merged, backward, filter_refs, f)
-    lay_toeplitz(rows, wide, lon_dev, merged, backward, f, t_ref, e_ref)
+    lay_toeplitz(others, wide, lon_dev, merged, backward, f, t_ref, e_ref)
 
     def put(values, first):
         values = values.T
@@ -200,7 +212,8 @@
     span = 2 * LANES
     for row in range(rows):
         window = xs[row : row + 3, :span, :].reshape(3 * span, height)
-        total = jnp.dot(t_ref[row], window, preferred_element_type=jnp.float32)
+        laid = ahead_ref[ahead.index(row)] if row in ahead else t_ref[others.index(row)]
+        total = jnp.dot(laid, window, preferred_element_type=jnp.float32)
         if row in wide:
             beyond = []
             for tap in range(3):
@@ -285,7 +298,17 @@
         filters = [above, own_filters, below]
     pool = (bands if merged else 3, *own_filters.shape)
 
-    def convolve(values, backward):
+    def lay(filters, backward):
+        wide = [row for row in range(rows) if tables[backward][row] == SMAX]
+        shape = (len(rows_ahead(rows, wide)[0]), kernels * lon_dev, 6 * LANES)
+        return pl.pallas_call(
+            partial(table_kernel, wide, rows, bands, lon_dev, merged, bool(backward)),
+            out_shape=jax.ShapeDtypeStruct(shape, BF16),
+            scratch_shapes=[pltpu.VMEM(pool, jnp.float32)],
+            compiler_params=SMALL,
+        )(*filters)
+
+    def convolve(values, laid, backward):
         values = values.reshape(segments, height, cells)
         halo = [] if merged else from_bands(values[0])
         return pl.pallas_call(
@@ -296,21 +319,23 @@
             out_shape=jax.ShapeDtypeStruct(values.shape, BF16),
             scratch_shapes=[
                 pltpu.VMEM(pool, jnp.float32),
-                pltpu.VMEM((rows, kernels * lon_dev, 6 * LANES), BF16),
+                pltpu.VMEM((rows - laid.shape[0], kernels * lon_dev, 6 * LANES), BF16),
                 pltpu.VMEM((tables[backward].count(SMAX), kernels * lon_dev, 3 * LANES), BF16),
                 pltpu.VMEM((rows + 2, (2 * SMAX + 1) * lon_dev, height), BF16),
                 pltpu.VMEM((rows * lon_dev, kernels * height), BF16),
             ],
             compiler_params=LARGE,
-        )(w_group, values, *filters, *halo)
-
-    mixed_in = exchange(convolve(columns, 0))
+        )(w_group, values, laid, *filters, *halo)
+
+    mixed_in = convolve(columns, lay(filters, 0), 0)
+    mixed_in, later = lax.optimization_barrier((mixed_in, filters))
+    mixed_in = exchange(mixed_in)
     outputs, grad_mixed = pl.pallas_call(
         dense_kernel,
         out_shape=(jax.ShapeDtypeStruct((cells, channels), BF16), square),
         compiler_params=SMALL,
     )(mixed_in.reshape(channels, cells), w_mix, grad_out.reshape(cells, channels))
-    grad_in = exchange(convolve(exchange(grad_mixed), 1))
+    grad_in = exchange(convolve(exchange(grad_mixed), lay(later, 1), 1))
     grad_in = transposed(grad_in.reshape(channels, cells))
     return outputs.reshape(inputs.shape), grad_in.reshape(inputs.shape)
 

time: 53.6 us -> 53.8 us (level)
  blocking collectives: 29.7 us -> 19.7 us
  waiting for transfers between devices: 7.58 us -> 13.4 us
  starting transfers between devices: 7.61 us -> 10.2 us
  local copies, waits for them, and re-layouts: 0.02 us -> 0.93 us
  Pallas kernels: 7.72 us -> 8.51 us
    all_to_all x3 -> x2, blocking collectives: 29.7 us -> 19.7 us  [exchange(): return lax.all_to_all(parted, everyone, 0, 0)]
    all_to_all x1 -> x2, waiting for transfers between devices: 6.46 us -> 12.1 us  [exchange(): return lax.all_to_all(parted, everyone, 0, 0)]
    all_to_all x1 -> x2, starting transfers between devices: 7.3 us -> 9.87 us  [exchange(): return lax.all_to_all(parted, everyone, 0, 0)]
    pallas_call x0 -> x2, Pallas kernels: none -> 1.14 us  [lay(): pl.pallas_call(partial(table_kernel, wide, rows, bands, lon_dev, merged,...]
    unnamed x8 -> x10, local copies, waits for them, and re-layouts: 0.02 us -> 0.93 us
  transfers between devices with their start and end apart: 2 -> 3, of which waited for: 2 -> 3; matrix products, arithmetic and copies ran while one was open for 0% -> 0% of each run, Pallas kernels for 0% -> 2%
where the time goes in v5:
time: 53.8 us; the launch traced here: 53.5 us
  blocking collectives  19.7 us (37%)
  waiting for transfers between devices  13.4 us (25%)
  starting transfers between devices  10.2 us (19%)
  Pallas kernels  8.51 us (16%)
  local copies, waits for them, and re-layouts  0.93 us (2%)
  between operations  0.71 us (1%)
    all_to_all x2, blocking collectives, exchange(): return lax.all_to_all(parted, everyone, 0, 0)  19.7 us
    all_to_all x2, waiting for transfers between devices, exchange(): return lax.all_to_all(parted, everyone, 0, 0)  12.1 us
    all_to_all x2, starting transfers between devices, exchange(): return lax.all_to_all(parted, everyone, 0, 0)  9.87 us
    pallas_call x2, Pallas kernels, convolve(): pl.pallas_call(partial(conv_kernel, tables[backward], bands, lon_dev, mer...  3.64 us
    pallas_call x1, Pallas kernels, body(): pl.pallas_call(partial(enter_kernel, lon_dev), out_shape=(square, jax.Sha...  1.8 us
    ppermute x1, waiting for transfers between devices, body(): filters = [own_filters, lax.ppermute(own_filters, 'lat', [(0, 1), (1, 0)])]  1.33 us
    pallas_call x1, Pallas kernels, body(): pl.pallas_call(dense_kernel, out_shape=(jax.ShapeDtypeStruct((cells, chan...  1.19 us
    pallas_call x2, Pallas kernels, lay(): pl.pallas_call(partial(table_kernel, wide, rows, bands, lon_dev, merged,...  1.14 us
  transfers between devices with their start and end apart: 3, of which 3 were waited for; matrix products, arithmetic and copies ran while one was open for 0% of the time, Pallas kernels for 2%

profile of v5, /device:TPU:0, one launch (start us, length us, event | category | flops | bytes accessed | tf_op | source)
XLA Modules:
  0.0 53.5 jit_solution(5162068868939251132)
XLA Ops:
  0.6 0.0 copy-start.4
  0.6 1.8 %shard_map.77 = (bf16[256,256]{1,0:T(8,128)(2,1)}, f32[4,3,8,384]{3,2,1,0:T(8,128)}) custom-call(s32[8]{0:T(128)} %w_ref.4, bf16[256,256]{1,0:T(8,128)(2,1)} %bitcast.21, f32[4,3,8,257]{3,2,1,0:T(8,128)} %bitcast.20), custom_call_target="tpu_custom_call" | custom-call | tf_op jit(solution)/shard_map/pallas_call | solution.py:281
  2.4 0.0 copy-start.1
  2.4 7.3 %all-to-all-start = ((bf16[32,8,256]{2,1,0:T(8,128)(2,1)}), bf16[32,8,256]{2,1,0:T(8,128)(2,1)S(1)}, u32[]{:S(2)}, u32[]{:S(2)}) async-start(bf16[32,8,256]{2,1,0:T(8,128)(2,1)} %bitcast.22), calls=%async_computation | async-start | bytes 262144 | tf_op jit(solution)/shard_map/all_to_all | solution.py:279
  9.7 0.3 collective-permute-start
  10.1 1.3 %collective-permute-done.refs_1_ = f32[4,3,8,384]{3,2,1,0:T(8,128)S(1)} collective-permute-done((f32[4,3,8,384]{3,2,1,0:T(8,128)}, f32[4,3,8,384]{3,2,1,0:T(8,128)S(1)}, u32[]{:S(2)}, u32[]{:S(2)}) %collective-permute-start) | collective-permute-done | bytes 147488 | tf_op jit(solution)/shard_map/ppermute | solution.py:295
  11.4 0.9 %copy-done = f32[4,3,8,384]{3,2,1,0:T(8,128)S(1)} copy-done((f32[4,3,8,384]{3,2,1,0:T(8,128)S(1)}, f32[4,3,8,384]{3,2,1,0:T(8,128)}, u32[]{:S(2)}) %copy-start) | copy-done | bytes 147480
  12.3 0.5 shard_map.78.ahead_ref
  12.8 0.0 copy-start.2
  12.8 0.0 copy-start.3
  12.8 4.8 %all-to-all-done = bf16[32,8,256]{2,1,0:T(8,128)(2,1)S(1)} async-done(((bf16[32,8,256]{2,1,0:T(8,128)(2,1)}), bf16[32,8,256]{2,1,0:T(8,128)(2,1)S(1)}, u32[]{:S(2)}, u32[]{:S(2)}) %all-to-all-start) | async-done | bytes 131104 | tf_op jit(solution)/shard_map/all_to_all | solution.py:279
  17.7 0.0 copy-done.4
  17.7 0.0 copy-done.1
  17.7 1.8 %shard_map.79 = bf16[2,128,256]{2,1,0:T(8,128)(2,1)S(1)} custom-call(bf16[4,4,256]{2,1,0:T(4,128)(2,1)S(1)} %copy-done.4, bf16[2,128,256]{2,1,0:T(8,128)(2,1)S(1)} %bitcast.13, bf16[8,128,768]{2,1,0:T(8,128)(2,1)S(1)} %shard_map.78.ahead_ref, f32[4,3,8,384]{3,2,1,0:T(8,128)S(1)} %copy-done.1, f32[4,3,8,384]{3,2,1,0:T(8,128)S(1)} %collective-permute-done.refs_1_), custom_call_target="tpu_custom_call" | custom-call | tf_op jit(solution)/shard_map/pallas_call | solution.py:314
  19.5 9.9 %all_to_all.20 = bf16[32,8,256]{2,1,0:T(8,128)(2,1)S(1)} all-to-all(bf16[32,8,256]{2,1,0:T(8,128)(2,1)S(1)} %bitcast.17), channel_id=1, replica_groups=mesh['lon'=16,'lat'=2] {'lat','lon'}, dimensions={0} | all-to-all | bytes 262144 | tf_op jit(solution)/shard_map/all_to_all | solution.py:279
  29.4 0.0 copy-done.2
  29.4 0.0 copy-done.3
  29.4 1.2 %shard_map.80 = (bf16[256,256]{1,0:T(8,128)(2,1)}, bf16[256,256]{1,0:T(8,128)(2,1)}) custom-call(bf16[256,256]{1,0:T(8,128)(2,1)S(1)} %bitcast.16, bf16[256,256]{1,0:T(8,128)(2,1)S(1)} %copy-done.2, bf16[256,256]{1,0:T(8,128)(2,1)S(1)} %bitcast.19), custom_call_target="tpu_custom_call" | custom-call | tf_op jit(solution)/shard_map/pallas_call | solution.py:333
  30.6 2.6 %all-to-all-start.2 = ((bf16[32,8,256]{2,1,0:T(8,128)(2,1)}), bf16[32,8,256]{2,1,0:T(8,128)(2,1)S(1)}, u32[]{:S(2)}, u32[]{:S(2)}) async-start(bf16[32,8,256]{2,1,0:T(8,128)(2,1)} %bitcast.8), calls=%async_computation.2 | async-start | bytes 262144 | tf_op jit(solution)/shard_map/all_to_all | solution.py:279
  33.2 0.6 %shard_map.81.ahead_ref = bf16[8,128,768]{2,1,0:T(8,128)(2,1)S(1)} custom-call(f32[4,3,8,384]{3,2,1,0:T(8,128)S(1)} %copy-done.1, f32[4,3,8,384]{3,2,1,0:T(8,128)S(1)} %collective-permute-done.refs_1_), custom_call_target="tpu_custom_call" | custom-call | tf_op jit(solution)/shard_map/pallas_call | solution.py:304
  33.8 7.3 %all-to-all-done.2 = bf16[32,8,256]{2,1,0:T(8,128)(2,1)S(1)} async-done(((bf16[32,8,256]{2,1,0:T(8,128)(2,1)}), bf16[32,8,256]{2,1,0:T(8,128)(2,1)S(1)}, u32[]{:S(2)}, u32[]{:S(2)}) %all-to-all-start.2) | async-done | bytes 131104 | tf_op jit(solution)/shard_map/all_to_all | solution.py:279
  41.1 1.9 %shard_map.82 = bf16[2,128,256]{2,1,0:T(8,128)(2,1)S(1)} custom-call(bf16[4,4,256]{2,1,0:T(4,128)(2,1)S(1)} %copy-done.4, bf16[2,128,256]{2,1,0:T(8,128)(2,1)S(1)} %bitcast.14, bf16[8,128,768]{2,1,0:T(8,128)(2,1)S(1)} %shard_map.81.ahead_ref, f32[4,3,8,384]{3,2,1,0:T(8,128)S(1)} %copy-done.1, f32[4,3,8,384]{3,2,1,0:T(8,128)S(1)} %collective-permute-done.refs_1_), custom_call_target="tpu_custom_call" | custom-call | tf_op jit(solution)/shard_map/pallas_call | solution.py:314
  42.9 9.8 %all_to_all.21 = bf16[32,8,256]{2,1,0:T(8,128)(2,1)S(1)} all-to-all(bf16[32,8,256]{2,1,0:T(8,128)(2,1)S(1)} %bitcast.15), channel_id=1, replica_groups=mesh['lon'=16,'lat'=2] {'lat','lon'}, dimensions={0} | all-to-all | bytes 262144 | tf_op jit(solution)/shard_map/all_to_all | solution.py:279
  52.7 0.7 %shard_map.83 = bf16[256,256]{1,0:T(8,128)(2,1)} custom-call(bf16[256,256]{1,0:T(8,128)(2,1)S(1)} %bitcast.18), custom_call_target="tpu_custom_call" | custom-call | tf_op jit(solution)/shard_map/pallas_call | solution.py:42
  (1 shorter events, 0.0 us)
Async XLA Ops:
  0.6 17.0 %copy-start.4 = (bf16[4,4,256]{2,1,0:T(4,128)(2,1)S(1)}, bf16[4,4,256]{2,1,0:T(4,128)(2,1)}, u32[]{:S(2)}) copy-start(bf16[4,4,256]{2,1,0:T(4,128)(2,1)} %w_ref.7) | copy-start | bytes 24580
  2.4 15.2 %copy-start.1 = (f32[4,3,8,384]{3,2,1,0:T(8,128)S(1)}, f32[4,3,8,384]{3,2,1,0:T(8,128)}, u32[]{:S(2)}) copy-start(f32[4,3,8,384]{3,2,1,0:T(8,128)} %get-tuple-element.14.refs_0_) | copy-start | bytes 442372
  2.4 15.2 %all-to-all-start = ((bf16[32,8,256]{2,1,0:T(8,128)(2,1)}), bf16[32,8,256]{2,1,0:T(8,128)(2,1)S(1)}, u32[]{:S(2)}, u32[]{:S(2)}) async-start(bf16[32,8,256]{2,1,0:T(8,128)(2,1)} %bitcast.22), calls=%async_computation | async-start | bytes 262144 | tf_op jit(solution)/shard_map/all_to_all | solution.py:279
  9.7 1.6 %collective-permute-start = (f32[4,3,8,384]{3,2,1,0:T(8,128)}, f32[4,3,8,384]{3,2,1,0:T(8,128)S(1)}, u32[]{:S(2)}, u32[]{:S(2)}) collective-permute-start(f32[4,3,8,384]{3,2,1,0:T(8,128)} %get-tuple-element.14.refs_0_), channel_id=1, source_target_pairs={{0,1},{1,0},{2,3},{3,2},{4,5},{5,4},{6,7},{7,6},{8,9},{9,8},{10,11... | collective-permute-start | bytes 442376 | tf_op jit(solution)/shard_map/ppermute | solution.py:295
  11.4 0.9 %copy-start = (f32[4,3,8,384]{3,2,1,0:T(8,128)S(1)}, f32[4,3,8,384]{3,2,1,0:T(8,128)}, u32[]{:S(2)}) copy-start(f32[4,3,8,384]{3,2,1,0:T(8,128)} %get-tuple-element.14.refs_0_) | copy-start | bytes 442372
  12.8 16.6 %copy-start.2 = (bf16[256,256]{1,0:T(8,128)(2,1)S(1)}, bf16[256,256]{1,0:T(8,128)(2,1)}, u32[]{:S(2)}) copy-start(bf16[256,256]{1,0:T(8,128)(2,1)} %w_ref.6) | copy-start | bytes 393220
  12.8 16.6 %copy-start.3 = (bf16[8,32,256]{2,1,0:T(8,128)(2,1)S(1)}, bf16[8,32,256]{2,1,0:T(8,128)(2,1)}, u32[]{:S(2)}) copy-start(bf16[8,32,256]{2,1,0:T(8,128)(2,1)} %param.11) | copy-start | bytes 393220
  30.6 10.5 %all-to-all-start.2 = ((bf16[32,8,256]{2,1,0:T(8,128)(2,1)}), bf16[32,8,256]{2,1,0:T(8,128)(2,1)S(1)}, u32[]{:S(2)}, u32[]{:S(2)}) async-start(bf16[32,8,256]{2,1,0:T(8,128)(2,1)} %bitcast.8), calls=%async_computation.2 | async-start | bytes 262144 | tf_op jit(solution)/shard_map/all_to_all | solution.py:279

commit v6 on v5

--- a/solution.py
+++ b/solution.py
@@ -162,10 +162,12 @@
     return ahead, [row for row in range(rows) if row not in ahead]
 
 
-def table_kernel(wide, rows, bands, lon_dev, merged, backward, *refs):
-    *filter_refs, t_ref, f = refs
-    collect(bands, merged, backward, filter_refs, f)
-    lay_toeplitz(rows_ahead(rows, wide)[0], wide, lon_dev, merged, backward, f, t_ref)
+def table_kernel(wides, rows, bands, lon_dev, merged, *refs):
+    *filter_refs, forward_ref, backward_ref, f = refs
+    for backward, t_ref in enumerate((forward_ref, backward_ref)):
+        wide = wides[backward]
+        collect(bands, merged, bool(backward), filter_refs, f)
+        lay_toeplitz(rows_ahead(rows, wide)[0], wide, lon_dev, merged, bool(backward), f, t_ref)
 
 
 def conv_kernel(
@@ -298,15 +300,18 @@
         filters = [above, own_filters, below]
     pool = (bands if merged else 3, *own_filters.shape)
 
-    def lay(filters, backward):
-        wide = [row for row in range(rows) if tables[backward][row] == SMAX]
-        shape = (len(rows_ahead(rows, wide)[0]), kernels * lon_dev, 6 * LANES)
-        return pl.pallas_call(
-            partial(table_kernel, wide, rows, bands, lon_dev, merged, bool(backward)),
-            out_shape=jax.ShapeDtypeStruct(shape, BF16),
-            scratch_shapes=[pltpu.VMEM(pool, jnp.float32)],
-            compiler_params=SMALL,
-        )(*filters)
+    wides = [[row for row in range(rows) if table[row] == SMAX] for table in tables]
+    laid = pl.pallas_call(
+        partial(table_kernel, wides, rows, bands, lon_dev, merged),
+        out_shape=[
+            jax.ShapeDtypeStruct(
+                (len(rows_ahead(rows, wide)[0]), kernels * lon_dev, 6 * LANES), BF16
+            )
+            for wide in wides
+        ],
+        scratch_shapes=[pltpu.VMEM(pool, jnp.float32)],
+        compiler_params=SMALL,
+    )(*filters)
 
     def convolve(values, laid, backward):
         values = values.reshape(segments, height, cells)
@@ -327,15 +332,13 @@
             compiler_params=LARGE,
         )(w_group, values, laid, *filters, *halo)
 
-    mixed_in = convolve(columns, lay(filters, 0), 0)
-    mixed_in, later = lax.optimization_barrier((mixed_in, filters))
-    mixed_in = exchange(mixed_in)
+    mixed_in = exchange(convolve(columns, laid[0], 0))
     outputs, grad_mixed = pl.pallas_call(
         dense_kernel,
         out_shape=(jax.ShapeDtypeStruct((cells, channels), BF16), square),
         compiler_params=SMALL,
     )(mixed_in.reshape(channels, cells), w_mix, grad_out.reshape(cells, channels))
-    grad_in = exchange(convolve(exchange(grad_mixed), lay(later, 1), 1))
+    grad_in = exchange(convolve(exchange(grad_mixed), laid[1], 1))
     grad_in = transposed(grad_in.reshape(channels, cells))
     return outputs.reshape(inputs.shape), grad_in.reshape(inputs.shape)
 

time: 53.8 us -> 54.7 us (1.017)
  blocking collectives: 19.7 us -> 29.7 us
  waiting for transfers between devices: 13.4 us -> 5.72 us
  starting transfers between devices: 10.2 us -> 7.61 us
  local copies, waits for them, and re-layouts: 0.93 us -> 2.52 us
    all_to_all x2 -> x3, blocking collectives: 19.7 us -> 29.7 us  [exchange(): return lax.all_to_all(parted, everyone, 0, 0)]
    all_to_all x2 -> x1, waiting for transfers between devices: 12.1 us -> 4.39 us  [exchange(): return lax.all_to_all(parted, everyone, 0, 0)]
    all_to_all x2 -> x1, starting transfers between devices: 9.87 us -> 7.3 us  [exchange(): return lax.all_to_all(parted, everyone, 0, 0)]
    unnamed x10, local copies, waits for them, and re-layouts: 0.93 us -> 2.52 us
    pallas_call x2 -> x1, Pallas kernels: 1.14 us -> 0.96 us  [body(): pl.pallas_call(partial(table_kernel, wides, rows, bands, lon_dev, merged)...]
  transfers between devices with their start and end apart: 3 -> 2, of which waited for: 3 -> 2; matrix products, arithmetic and copies ran while one was open for 0% -> 0% of each run, Pallas kernels for 2% -> 2%
where the time goes in v6:
time: 54.7 us; the launch traced here: 54.3 us
  blocking collectives  29.7 us (54%)
  Pallas kernels  8.08 us (15%)
  starting transfers between devices  7.61 us (14%)
  waiting for transfers between devices  5.72 us (10%)
  local copies, waits for them, and re-layouts  2.52 us (5%)
  between operations  0.68 us (1%)
    all_to_all x3, blocking collectives, exchange(): return lax.all_to_all(parted, everyone, 0, 0)  29.7 us
    all_to_all x1, starting transfers between devices, exchange(): return lax.all_to_all(parted, everyone, 0, 0)  7.3 us
    all_to_all x1, waiting for transfers between devices, exchange(): return lax.all_to_all(parted, everyone, 0, 0)  4.39 us
    pallas_call x2, Pallas kernels, convolve(): pl.pallas_call(partial(conv_kernel, tables[backward], bands, lon_dev, mer...  3.53 us
    unnamed x10, local copies, waits for them, and re-layouts  2.52 us
    pallas_call x1, Pallas kernels, body(): pl.pallas_call(partial(enter_kernel, lon_dev), out_shape=(square, jax.Sha...  1.83 us
    ppermute x1, waiting for transfers between devices, body(): filters = [own_filters, lax.ppermute(own_filters, 'lat', [(0, 1), (1, 0)])]  1.33 us
  transfers between devices with their start and end apart: 2, of which 2 were waited for; matrix products, arithmetic and copies ran while one was open for 0% of the time, Pallas kernels for 2%

profile of v6, /device:TPU:0, one launch (start us, length us, event | category | flops | bytes accessed | tf_op | source)
XLA Modules:
  0.0 54.3 jit_solution(3660637259322334323)
XLA Ops:
  0.6 0.0 copy-start.2
  0.6 1.8 %shard_map.77 = (bf16[256,256]{1,0:T(8,128)(2,1)}, f32[4,3,8,384]{3,2,1,0:T(8,128)}) custom-call(s32[8]{0:T(128)} %w_ref.4, bf16[256,256]{1,0:T(8,128)(2,1)} %bitcast.22, f32[4,3,8,257]{3,2,1,0:T(8,128)} %bitcast.21), custom_call_target="tpu_custom_call" | custom-call | tf_op jit(solution)/shard_map/pallas_call | solution.py:283
  2.5 7.3 %all-to-all-start = ((bf16[32,8,256]{2,1,0:T(8,128)(2,1)}), bf16[32,8,256]{2,1,0:T(8,128)(2,1)S(1)}, u32[]{:S(2)}, u32[]{:S(2)}) async-start(bf16[32,8,256]{2,1,0:T(8,128)(2,1)} %bitcast.23), calls=%async_computation | async-start | bytes 262144 | tf_op jit(solution)/shard_map/all_to_all | solution.py:281
  9.8 0.3 collective-permute-start
  10.1 1.3 %collective-permute-done.refs_1_ = f32[4,3,8,384]{3,2,1,0:T(8,128)S(1)} collective-permute-done((f32[4,3,8,384]{3,2,1,0:T(8,128)}, f32[4,3,8,384]{3,2,1,0:T(8,128)S(1)}, u32[]{:S(2)}, u32[]{:S(2)}) %collective-permute-start) | collective-permute-done | bytes 147488 | tf_op jit(solution)/shard_map/ppermute | solution.py:297
  11.4 0.0 copy-start
  11.4 0.9 %copy-done = f32[4,3,8,384]{3,2,1,0:T(8,128)S(1)} copy-done((f32[4,3,8,384]{3,2,1,0:T(8,128)S(1)}, f32[4,3,8,384]{3,2,1,0:T(8,128)}, u32[]{:S(2)}) %copy-start) | copy-done | bytes 147480
  12.3 1.0 %shard_map.78 = (bf16[8,128,768]{2,1,0:T(8,128)(2,1)S(1)}, bf16[8,128,768]{2,1,0:T(8,128)(2,1)S(1)}) custom-call(f32[4,3,8,384]{3,2,1,0:T(8,128)S(1)} %copy-done, f32[4,3,8,384]{3,2,1,0:T(8,128)S(1)} %collective-permute-done.refs_1_), custom_call_target="tpu_custom_call" | custom-call | tf_op jit(solution)/shard_map/pallas_call | solution.py:304
  13.3 4.4 %all-to-all-done = bf16[32,8,256]{2,1,0:T(8,128)(2,1)S(1)} async-done(((bf16[32,8,256]{2,1,0:T(8,128)(2,1)}), bf16[32,8,256]{2,1,0:T(8,128)(2,1)S(1)}, u32[]{:S(2)}, u32[]{:S(2)}) %all-to-all-start) | async-done | bytes 131104 | tf_op jit(solution)/shard_map/all_to_all | solution.py:281
  17.7 0.0 copy-start.1
  17.7 0.9 %copy-done.1 = f32[4,3,8,384]{3,2,1,0:T(8,128)S(1)} copy-done((f32[4,3,8,384]{3,2,1,0:T(8,128)S(1)}, f32[4,3,8,384]{3,2,1,0:T(8,128)}, u32[]{:S(2)}) %copy-start.1) | copy-done | bytes 147480
  18.6 0.0 copy-start.4
  18.6 0.7 %copy-done.4 = bf16[4,4,256]{2,1,0:T(4,128)(2,1)S(1)} copy-done((bf16[4,4,256]{2,1,0:T(4,128)(2,1)S(1)}, bf16[4,4,256]{2,1,0:T(4,128)(2,1)}, u32[]{:S(2)}) %copy-start.4) | copy-done | bytes 8216
  19.3 0.0 copy-start.3
  19.3 1.7 %shard_map.79 = bf16[2,128,256]{2,1,0:T(8,128)(2,1)S(1)} custom-call(bf16[4,4,256]{2,1,0:T(4,128)(2,1)S(1)} %copy-done.4, bf16[2,128,256]{2,1,0:T(8,128)(2,1)S(1)} %bitcast.13, bf16[8,128,768]{2,1,0:T(8,128)(2,1)S(1)} %get-tuple-element.10.ahead_ref, f32[4,3,8,384]{3,2,1,0:T(8,128)S(1)} %copy-done.1, f32[4,3,8,384]{3,2,1,0:T(8,128)S(1)} %collective-permute-done.refs_1_), custom_call_target="tpu_custom_call" | custom-call | tf_op jit(solution)/shard_map/pallas_call | solution.py:319
  21.0 9.9 %all_to_all.20 = bf16[32,8,256]{2,1,0:T(8,128)(2,1)S(1)} all-to-all(bf16[32,8,256]{2,1,0:T(8,128)(2,1)S(1)} %bitcast.17), channel_id=1, replica_groups=mesh['lon'=16,'lat'=2] {'lat','lon'}, dimensions={0} | all-to-all | bytes 262144 | tf_op jit(solution)/shard_map/all_to_all | solution.py:281
  31.0 0.0 copy-done.2
  31.0 0.0 copy-done.3
  31.0 1.0 %shard_map.80 = (bf16[256,256]{1,0:T(8,128)(2,1)}, bf16[256,256]{1,0:T(8,128)(2,1)S(1)}) custom-call(bf16[256,256]{1,0:T(8,128)(2,1)S(1)} %bitcast.16, bf16[256,256]{1,0:T(8,128)(2,1)S(1)} %copy-done.2, bf16[256,256]{1,0:T(8,128)(2,1)S(1)} %bitcast.19), custom_call_target="tpu_custom_call" | custom-call | tf_op jit(solution)/shard_map/pallas_call | solution.py:336
  32.0 9.9 %all_to_all.21 = bf16[32,8,256]{2,1,0:T(8,128)(2,1)S(1)} all-to-all(bf16[32,8,256]{2,1,0:T(8,128)(2,1)S(1)} %bitcast.20), channel_id=1, replica_groups=mesh['lon'=16,'lat'=2] {'lat','lon'}, dimensions={0} | all-to-all | bytes 262144 | tf_op jit(solution)/shard_map/all_to_all | solution.py:281
  41.9 1.8 %shard_map.81 = bf16[2,128,256]{2,1,0:T(8,128)(2,1)S(1)} custom-call(bf16[4,4,256]{2,1,0:T(4,128)(2,1)S(1)} %copy-done.4, bf16[2,128,256]{2,1,0:T(8,128)(2,1)S(1)} %bitcast.14, bf16[8,128,768]{2,1,0:T(8,128)(2,1)S(1)} %get-tuple-element.13.ahead_ref, f32[4,3,8,384]{3,2,1,0:T(8,128)S(1)} %copy-done.1, f32[4,3,8,384]{3,2,1,0:T(8,128)S(1)} %collective-permute-done.refs_1_), custom_call_target="tpu_custom_call" | custom-call | tf_op jit(solution)/shard_map/pallas_call | solution.py:319
  43.7 9.9 %all_to_all.22 = bf16[32,8,256]{2,1,0:T(8,128)(2,1)S(1)} all-to-all(bf16[32,8,256]{2,1,0:T(8,128)(2,1)S(1)} %bitcast.15), channel_id=1, replica_groups=mesh['lon'=16,'lat'=2] {'lat','lon'}, dimensions={0} | all-to-all | bytes 262144 | tf_op jit(solution)/shard_map/all_to_all | solution.py:281
  53.6 0.7 %shard_map.82 = bf16[256,256]{1,0:T(8,128)(2,1)} custom-call(bf16[256,256]{1,0:T(8,128)(2,1)S(1)} %bitcast.18), custom_call_target="tpu_custom_call" | custom-call | tf_op jit(solution)/shard_map/pallas_call | solution.py:42
Async XLA Ops:
  0.6 30.3 %copy-start.2 = (bf16[256,256]{1,0:T(8,128)(2,1)S(1)}, bf16[256,256]{1,0:T(8,128)(2,1)}, u32[]{:S(2)}) copy-start(bf16[256,256]{1,0:T(8,128)(2,1)} %w_ref.6) | copy-start | bytes 393220
  2.5 15.2 %all-to-all-start = ((bf16[32,8,256]{2,1,0:T(8,128)(2,1)}), bf16[32,8,256]{2,1,0:T(8,128)(2,1)S(1)}, u32[]{:S(2)}, u32[]{:S(2)}) async-start(bf16[32,8,256]{2,1,0:T(8,128)(2,1)} %bitcast.23), calls=%async_computation | async-start | bytes 262144 | tf_op jit(solution)/shard_map/all_to_all | solution.py:281
  9.8 1.6 %collective-permute-start = (f32[4,3,8,384]{3,2,1,0:T(8,128)}, f32[4,3,8,384]{3,2,1,0:T(8,128)S(1)}, u32[]{:S(2)}, u32[]{:S(2)}) collective-permute-start(f32[4,3,8,384]{3,2,1,0:T(8,128)} %get-tuple-element.9.refs_0_), channel_id=1, source_target_pairs={{0,1},{1,0},{2,3},{3,2},{4,5},{5,4},{6,7},{7,6},{8,9},{9,8},{10,11... | collective-permute-start | bytes 442376 | tf_op jit(solution)/shard_map/ppermute | solution.py:297
  11.4 0.9 %copy-start = (f32[4,3,8,384]{3,2,1,0:T(8,128)S(1)}, f32[4,3,8,384]{3,2,1,0:T(8,128)}, u32[]{:S(2)}) copy-start(f32[4,3,8,384]{3,2,1,0:T(8,128)} %get-tuple-element.9.refs_0_) | copy-start | bytes 442372
  17.7 0.9 %copy-start.1 = (f32[4,3,8,384]{3,2,1,0:T(8,128)S(1)}, f32[4,3,8,384]{3,2,1,0:T(8,128)}, u32[]{:S(2)}) copy-start(f32[4,3,8,384]{3,2,1,0:T(8,128)} %get-tuple-element.9.refs_0_) | copy-start | bytes 442372
  18.6 0.7 %copy-start.4 = (bf16[4,4,256]{2,1,0:T(4,128)(2,1)S(1)}, bf16[4,4,256]{2,1,0:T(4,128)(2,1)}, u32[]{:S(2)}) copy-start(bf16[4,4,256]{2,1,0:T(4,128)(2,1)} %w_ref.7) | copy-start | bytes 24580
  19.3 11.7 %copy-start.3 = (bf16[8,32,256]{2,1,0:T(8,128)(2,1)S(1)}, bf16[8,32,256]{2,1,0:T(8,128)(2,1)}, u32[]{:S(2)}) copy-start(bf16[8,32,256]{2,1,0:T(8,128)(2,1)} %param.11) | copy-start | bytes 393220

commit v7 on v4

--- a/solution.py
+++ b/solution.py
@@ -88,13 +88,13 @@
             f[segment] = values.reshape(kernels, taps, lines, width)
 
 
-def lay_toeplitz(rows, wide, lon_dev, merged, backward, f, t_ref, e_ref):
+def lay_toeplitz(rows, wide, lon_dev, merged, backward, f, t_ref, e_ref=None):
     segments, kernels, _, held, _ = f.shape
     shape = (lon_dev, LANES)
     lane, line = iota(shape, 1), iota(shape, 0)
     upper = lane >= line
     corner = lane == line
-    for row in range(rows):
+    for place, row in enumerate(rows):
         for tap in range(3):
             source, column = (row + tap - 1, 2 - tap) if backward else (row, tap)
             source += 0 if merged else held
@@ -114,8 +114,8 @@
                 else:
                     parts = [jnp.zeros(shape, jnp.float32)] * 2
                 for i, part in enumerate(parts):
-                    t_ref[row, here, pl.ds((tap * 2 + i) * LANES, LANES)] = part.astype(BF16)
-                if row in wide:
+                    t_ref[place, here, pl.ds((tap * 2 + i) * LANES, LANES)] = part.astype(BF16)
+                if e_ref is not None and row in wide:
                     last = parts[0]
                     if present:
                         last = jnp.where(corner, turned(2), jnp.where(upper, 0.0, second))
@@ -157,9 +157,23 @@
     return jnp.where(same, spread, 0.0).astype(BF16)
 
 
+def rows_ahead(rows, wide, backward):
+    middle = () if backward else range(rows // 4, rows - rows // 4)
+    ahead = [row for row in middle if row not in wide]
+    return ahead, [row for row in range(rows) if row not in ahead]
+
+
+def table_kernel(wide, rows, bands, lon_dev, merged, *refs):
+    *filter_refs, t_ref, f = refs
+    collect(bands, merged, False, filter_refs, f)
+    lay_toeplitz(rows_ahead(rows, wide, False)[0], wide, lon_dev, merged, False, f, t_ref)
+
+
 def conv_kernel(
     table, bands, lon_dev, merged, everyone, share, backward, w_ref, own_ref, *refs
 ):
+    if not backward:
+        ahead_ref, *refs = refs
     count = 2 if merged else 3
     filter_refs, refs = refs[:count], refs[count:]
     *halo_refs, o_ref, f, t_ref, e_ref, xs, z_ref = refs
@@ -168,8 +182,9 @@
     held = rows // segments
     kernels = f.shape[1]
     wide = [row for row, reach in enumerate(table) if reach == SMAX]
+    ahead, others = rows_ahead(rows, wide, backward)
     collect(bands, merged, backward, filter_refs, f)
-    lay_toeplitz(rows, wide, lon_dev, merged, backward, f, t_ref, e_ref)
+    lay_toeplitz(others, wide, lon_dev, merged, backward, f, t_ref, e_ref)
 
     def put(values, first):
         values = values.T
@@ -200,7 +215,8 @@
     span = 2 * LANES
     for row in range(rows):
         window = xs[row : row + 3, :span, :].reshape(3 * span, height)
-        total = jnp.dot(t_ref[row], window, preferred_element_type=jnp.float32)
+        laid = ahead_ref[ahead.index(row)] if row in ahead else t_ref[others.index(row)]
+        total = jnp.dot(laid, window, preferred_element_type=jnp.float32)
         if row in wide:
             beyond = []
             for tap in range(3):
@@ -285,32 +301,41 @@
         filters = [above, own_filters, below]
     pool = (bands if merged else 3, *own_filters.shape)
 
-    def convolve(values, backward):
+    widest = [row for row in range(rows) if tables[0][row] == SMAX]
+    ahead = len(rows_ahead(rows, widest, False)[0])
+    laid = pl.pallas_call(
+        partial(table_kernel, widest, rows, bands, lon_dev, merged),
+        out_shape=jax.ShapeDtypeStruct((ahead, kernels * lon_dev, 6 * LANES), BF16),
+        scratch_shapes=[pltpu.VMEM(pool, jnp.float32)],
+        compiler_params=SMALL,
+    )(*filters)
+
+    def convolve(values, laid):
+        backward = not laid
         values = values.reshape(segments, height, cells)
         halo = [] if merged else from_bands(values[0])
         return pl.pallas_call(
             partial(
-                conv_kernel, tables[backward], bands, lon_dev, merged, everyone, share,
-                bool(backward),
+                conv_kernel, tables[backward], bands, lon_dev, merged, everyone, share, backward
             ),
             out_shape=jax.ShapeDtypeStruct(values.shape, BF16),
             scratch_shapes=[
                 pltpu.VMEM(pool, jnp.float32),
-                pltpu.VMEM((rows, kernels * lon_dev, 6 * LANES), BF16),
+                pltpu.VMEM((rows - ahead * len(laid), kernels * lon_dev, 6 * LANES), BF16),
                 pltpu.VMEM((tables[backward].count(SMAX), kernels * lon_dev, 3 * LANES), BF16),
                 pltpu.VMEM((rows + 2, (2 * SMAX + 1) * lon_dev, height), BF16),
                 pltpu.VMEM((rows * lon_dev, kernels * height), BF16),
             ],
             compiler_params=LARGE,
-        )(w_group, values, *filters, *halo)
-
-    mixed_in = exchange(convolve(columns, 0))
+        )(w_group, values, *laid, *filters, *halo)
+
+    mixed_in = exchange(convolve(columns, [laid]))
     outputs, grad_mixed = pl.pallas_call(
         dense_kernel,
         out_shape=(jax.ShapeDtypeStruct((cells, channels), BF16), square),
         compiler_params=SMALL,
     )(mixed_in.reshape(channels, cells), w_mix, grad_out.reshape(cells, channels))
-    grad_in = exchange(convolve(exchange(grad_mixed), 1))
+    grad_in = exchange(convolve(exchange(grad_mixed), []))
     grad_in = transposed(grad_in.reshape(channels, cells))
     return outputs.reshape(inputs.shape), grad_in.reshape(inputs.shape)
 

time: 53.6 us -> 53.4 us (level)
  waiting for transfers between devices: 7.58 us -> 6.15 us
  local copies, waits for them, and re-layouts: 0.02 us -> 0.93 us
    all_to_all x1, waiting for transfers between devices: 6.46 us -> 4.82 us  [exchange(): return lax.all_to_all(parted, everyone, 0, 0)]
    unnamed x8 -> x10, local copies, waits for them, and re-layouts: 0.02 us -> 0.93 us
  transfers between devices with their start and end apart: 2 -> 2, of which waited for: 2 -> 2; matrix products, arithmetic and copies ran while one was open for 0% -> 0% of each run, Pallas kernels for 0% -> 1%
where the time goes in v7:
time: 53.4 us; the launch traced here: 53.1 us
  blocking collectives  29.7 us (56%)
  Pallas kernels  7.98 us (15%)
  starting transfers between devices  7.61 us (14%)
  waiting for transfers between devices  6.15 us (12%)
  local copies, waits for them, and re-layouts  0.93 us (2%)
  between operations  0.69 us (1%)
    all_to_all x3, blocking collectives, exchange(): return lax.all_to_all(parted, everyone, 0, 0)  29.7 us
    all_to_all x1, starting transfers between devices, exchange(): return lax.all_to_all(parted, everyone, 0, 0)  7.3 us
    all_to_all x1, waiting for transfers between devices, exchange(): return lax.all_to_all(parted, everyone, 0, 0)  4.82 us
    pallas_call x2, Pallas kernels, convolve(): pl.pallas_call(partial(conv_kernel, tables[backward], bands, lon_dev, mer...  3.93 us
    pallas_call x1, Pallas kernels, body(): pl.pallas_call(partial(enter_kernel, lon_dev), out_shape=(square, jax.Sha...  1.8 us
    ppermute x1, waiting for transfers between devices, body(): filters = [own_filters, lax.ppermute(own_filters, 'lat', [(0, 1), (1, 0)])]  1.33 us
  transfers between devices with their start and end apart: 2, of which 2 were waited for; matrix products, arithmetic and copies ran while one was open for 0% of the time, Pallas kernels for 1%

profile of v7, /device:TPU:0, one launch (start us, length us, event | category | flops | bytes accessed | tf_op | source)
XLA Modules:
  0.0 53.1 jit_solution(3340126989697277286)
XLA Ops:
  0.6 0.0 copy-start.4
  0.6 1.8 %shard_map.77 = (bf16[256,256]{1,0:T(8,128)(2,1)}, f32[4,3,8,384]{3,2,1,0:T(8,128)}) custom-call(s32[8]{0:T(128)} %w_ref.4, bf16[256,256]{1,0:T(8,128)(2,1)} %bitcast.22, f32[4,3,8,257]{3,2,1,0:T(8,128)} %bitcast.21), custom_call_target="tpu_custom_call" | custom-call | tf_op jit(solution)/shard_map/pallas_call | solution.py:284
  2.4 0.0 copy-start.1
  2.4 7.3 %all-to-all-start = ((bf16[32,8,256]{2,1,0:T(8,128)(2,1)}), bf16[32,8,256]{2,1,0:T(8,128)(2,1)S(1)}, u32[]{:S(2)}, u32[]{:S(2)}) async-start(bf16[32,8,256]{2,1,0:T(8,128)(2,1)} %bitcast.23), calls=%async_computation | async-start | bytes 262144 | tf_op jit(solution)/shard_map/all_to_all | solution.py:282
  9.7 0.3 collective-permute-start
  10.1 1.3 %collective-permute-done.refs_1_.refs_2_ = f32[4,3,8,384]{3,2,1,0:T(8,128)S(1)} collective-permute-done((f32[4,3,8,384]{3,2,1,0:T(8,128)}, f32[4,3,8,384]{3,2,1,0:T(8,128)S(1)}, u32[]{:S(2)}, u32[]{:S(2)}) %collective-permute-start) | collective-permute-done | bytes 147488 | tf_op jit(solution)/shard_map/ppermute | solution.py:298
  11.4 0.0 copy-start
  11.4 0.9 %copy-done = f32[4,3,8,384]{3,2,1,0:T(8,128)S(1)} copy-done((f32[4,3,8,384]{3,2,1,0:T(8,128)S(1)}, f32[4,3,8,384]{3,2,1,0:T(8,128)}, u32[]{:S(2)}) %copy-start) | copy-done | bytes 147480
  12.3 0.5 shard_map.78.refs_0_
  12.8 0.0 copy-start.2
  12.8 0.0 copy-start.3
  12.8 4.8 %all-to-all-done = bf16[32,8,256]{2,1,0:T(8,128)(2,1)S(1)} async-done(((bf16[32,8,256]{2,1,0:T(8,128)(2,1)}), bf16[32,8,256]{2,1,0:T(8,128)(2,1)S(1)}, u32[]{:S(2)}, u32[]{:S(2)}) %all-to-all-start) | async-done | bytes 131104 | tf_op jit(solution)/shard_map/all_to_all | solution.py:282
  17.7 0.0 copy-done.4
  17.7 0.0 copy-done.1
  17.7 1.8 %shard_map.79 = bf16[2,128,256]{2,1,0:T(8,128)(2,1)S(1)} custom-call(bf16[4,4,256]{2,1,0:T(4,128)(2,1)S(1)} %copy-done.4, bf16[2,128,256]{2,1,0:T(8,128)(2,1)S(1)} %bitcast.13, bf16[8,128,768]{2,1,0:T(8,128)(2,1)S(1)} %shard_map.78.refs_0_, f32[4,3,8,384]{3,2,1,0:T(8,128)S(1)} %copy-done.1, f32[4,3,8,384]{3,2,1,0:T(8,128)S(1)} %collective-permute-done.refs_1_.refs_2_), custom_call_target="tpu_custom_call" | custom-call | tf_op jit(solution)/shard_map/pallas_call | solution.py:317
  19.5 9.9 %all_to_all.20 = bf16[32,8,256]{2,1,0:T(8,128)(2,1)S(1)} all-to-all(bf16[32,8,256]{2,1,0:T(8,128)(2,1)S(1)} %bitcast.17), channel_id=1, replica_groups=mesh['lon'=16,'lat'=2] {'lat','lon'}, dimensions={0} | all-to-all | bytes 262144 | tf_op jit(solution)/shard_map/all_to_all | solution.py:282
  29.4 0.0 copy-done.2
  29.4 0.0 copy-done.3
  29.4 1.0 %shard_map.80 = (bf16[256,256]{1,0:T(8,128)(2,1)}, bf16[256,256]{1,0:T(8,128)(2,1)S(1)}) custom-call(bf16[256,256]{1,0:T(8,128)(2,1)S(1)} %bitcast.14, bf16[256,256]{1,0:T(8,128)(2,1)S(1)} %copy-done.2, bf16[256,256]{1,0:T(8,128)(2,1)S(1)} %bitcast.19), custom_call_target="tpu_custom_call" | custom-call | tf_op jit(solution)/shard_map/pallas_call | solution.py:333
  30.4 9.9 %all_to_all.21 = bf16[32,8,256]{2,1,0:T(8,128)(2,1)S(1)} all-to-all(bf16[32,8,256]{2,1,0:T(8,128)(2,1)S(1)} %bitcast.20), channel_id=1, replica_groups=mesh['lon'=16,'lat'=2] {'lat','lon'}, dimensions={0} | all-to-all | bytes 262144 | tf_op jit(solution)/shard_map/all_to_all | solution.py:282
  40.3 2.1 %shard_map.81 = bf16[2,128,256]{2,1,0:T(8,128)(2,1)S(1)} custom-call(bf16[4,4,256]{2,1,0:T(4,128)(2,1)S(1)} %copy-done.4, bf16[2,128,256]{2,1,0:T(8,128)(2,1)S(1)} %bitcast.15, f32[4,3,8,384]{3,2,1,0:T(8,128)S(1)} %copy-done.1, f32[4,3,8,384]{3,2,1,0:T(8,128)S(1)} %collective-permute-done.refs_1_.refs_2_), custom_call_target="tpu_custom_call" | custom-call | tf_op jit(solution)/shard_map/pallas_call | solution.py:317
  42.4 9.9 %all_to_all.22 = bf16[32,8,256]{2,1,0:T(8,128)(2,1)S(1)} all-to-all(bf16[32,8,256]{2,1,0:T(8,128)(2,1)S(1)} %bitcast.16), channel_id=1, replica_groups=mesh['lon'=16,'lat'=2] {'lat','lon'}, dimensions={0} | all-to-all | bytes 262144 | tf_op jit(solution)/shard_map/all_to_all | solution.py:282
  52.4 0.7 %shard_map.82 = bf16[256,256]{1,0:T(8,128)(2,1)} custom-call(bf16[256,256]{1,0:T(8,128)(2,1)S(1)} %bitcast.18), custom_call_target="tpu_custom_call" | custom-call | tf_op jit(solution)/shard_map/pallas_call | solution.py:42
Async XLA Ops:
  0.6 17.0 %copy-start.4 = (bf16[4,4,256]{2,1,0:T(4,128)(2,1)S(1)}, bf16[4,4,256]{2,1,0:T(4,128)(2,1)}, u32[]{:S(2)}) copy-start(bf16[4,4,256]{2,1,0:T(4,128)(2,1)} %w_ref.7) | copy-start | bytes 24580
  2.4 15.2 %copy-start.1 = (f32[4,3,8,384]{3,2,1,0:T(8,128)S(1)}, f32[4,3,8,384]{3,2,1,0:T(8,128)}, u32[]{:S(2)}) copy-start(f32[4,3,8,384]{3,2,1,0:T(8,128)} %get-tuple-element.7.refs_0_.refs_1_) | copy-start | bytes 442372
  2.4 15.2 %all-to-all-start = ((bf16[32,8,256]{2,1,0:T(8,128)(2,1)}), bf16[32,8,256]{2,1,0:T(8,128)(2,1)S(1)}, u32[]{:S(2)}, u32[]{:S(2)}) async-start(bf16[32,8,256]{2,1,0:T(8,128)(2,1)} %bitcast.23), calls=%async_computation | async-start | bytes 262144 | tf_op jit(solution)/shard_map/all_to_all | solution.py:282
  9.7 1.6 %collective-permute-start = (f32[4,3,8,384]{3,2,1,0:T(8,128)}, f32[4,3,8,384]{3,2,1,0:T(8,128)S(1)}, u32[]{:S(2)}, u32[]{:S(2)}) collective-permute-start(f32[4,3,8,384]{3,2,1,0:T(8,128)} %get-tuple-element.7.refs_0_.refs_1_), channel_id=1, source_target_pairs={{0,1},{1,0},{2,3},{3,2},{4,5},{5,4},{6,7},{7,6},{8,9},{9,8},{10,11... | collective-permute-start | bytes 442376 | tf_op jit(solution)/shard_map/ppermute | solution.py:298
  11.4 0.9 %copy-start = (f32[4,3,8,384]{3,2,1,0:T(8,128)S(1)}, f32[4,3,8,384]{3,2,1,0:T(8,128)}, u32[]{:S(2)}) copy-start(f32[4,3,8,384]{3,2,1,0:T(8,128)} %get-tuple-element.7.refs_0_.refs_1_) | copy-start | bytes 442372
  12.8 16.6 %copy-start.2 = (bf16[256,256]{1,0:T(8,128)(2,1)S(1)}, bf16[256,256]{1,0:T(8,128)(2,1)}, u32[]{:S(2)}) copy-start(bf16[256,256]{1,0:T(8,128)(2,1)} %w_ref.6) | copy-start | bytes 393220
  12.8 16.6 %copy-start.3 = (bf16[8,32,256]{2,1,0:T(8,128)(2,1)S(1)}, bf16[8,32,256]{2,1,0:T(8,128)(2,1)}, u32[]{:S(2)}) copy-start(bf16[8,32,256]{2,1,0:T(8,128)(2,1)} %param.11) | copy-start | bytes 393220

commit v8 on v7

--- a/solution.py
+++ b/solution.py
@@ -158,8 +158,7 @@
 
 
 def rows_ahead(rows, wide, backward):
-    middle = () if backward else range(rows // 4, rows - rows // 4)
-    ahead = [row for row in middle if row not in wide]
+    ahead = [] if backward else [row for row in range(rows) if row not in wide]
     return ahead, [row for row in range(rows) if row not in ahead]
 
 

time: 53.4 us -> 53.3 us (level)
  no operation moved by 1% of the time
where the time goes in v8:
time: 53.3 us; the launch traced here: 53 us
  blocking collectives  29.7 us (56%)
  Pallas kernels  8.12 us (15%)
  starting transfers between devices  7.61 us (14%)
  waiting for transfers between devices  5.97 us (11%)
  local copies, waits for them, and re-layouts  0.93 us (2%)
  between operations  0.68 us (1%)
    all_to_all x3, blocking collectives, exchange(): return lax.all_to_all(parted, everyone, 0, 0)  29.7 us
    all_to_all x1, starting transfers between devices, exchange(): return lax.all_to_all(parted, everyone, 0, 0)  7.3 us
    all_to_all x1, waiting for transfers between devices, exchange(): return lax.all_to_all(parted, everyone, 0, 0)  4.64 us
    pallas_call x2, Pallas kernels, convolve(): pl.pallas_call(partial(conv_kernel, tables[backward], bands, lon_dev, mer...  3.87 us
    pallas_call x1, Pallas kernels, body(): pl.pallas_call(partial(enter_kernel, lon_dev), out_shape=(square, jax.Sha...  1.8 us
    ppermute x1, waiting for transfers between devices, body(): filters = [own_filters, lax.ppermute(own_filters, 'lat', [(0, 1), (1, 0)])]  1.33 us
  transfers between devices with their start and end apart: 2, of which 2 were waited for; matrix products, arithmetic and copies ran while one was open for 0% of the time, Pallas kernels for 1%

profile of v8, /device:TPU:0, one launch (start us, length us, event | category | flops | bytes accessed | tf_op | source)
XLA Modules:
  0.0 53.0 jit_solution(1504362087112706206)
XLA Ops:
  0.6 0.0 copy-start.4
  0.6 1.8 %shard_map.77 = (bf16[256,256]{1,0:T(8,128)(2,1)}, f32[4,3,8,384]{3,2,1,0:T(8,128)}) custom-call(s32[8]{0:T(128)} %w_ref.4, bf16[256,256]{1,0:T(8,128)(2,1)} %bitcast.22, f32[4,3,8,257]{3,2,1,0:T(8,128)} %bitcast.21), custom_call_target="tpu_custom_call" | custom-call | tf_op jit(solution)/shard_map/pallas_call | solution.py:283
  2.4 0.0 copy-start.1
  2.4 7.3 %all-to-all-start = ((bf16[32,8,256]{2,1,0:T(8,128)(2,1)}), bf16[32,8,256]{2,1,0:T(8,128)(2,1)S(1)}, u32[]{:S(2)}, u32[]{:S(2)}) async-start(bf16[32,8,256]{2,1,0:T(8,128)(2,1)} %bitcast.23), calls=%async_computation | async-start | bytes 262144 | tf_op jit(solution)/shard_map/all_to_all | solution.py:281
  9.7 0.3 collective-permute-start
  10.1 1.3 %collective-permute-done.refs_1_.refs_2_ = f32[4,3,8,384]{3,2,1,0:T(8,128)S(1)} collective-permute-done((f32[4,3,8,384]{3,2,1,0:T(8,128)}, f32[4,3,8,384]{3,2,1,0:T(8,128)S(1)}, u32[]{:S(2)}, u32[]{:S(2)}) %collective-permute-start) | collective-permute-done | bytes 147488 | tf_op jit(solution)/shard_map/ppermute | solution.py:297
  11.4 0.0 copy-start
  11.4 0.9 %copy-done = f32[4,3,8,384]{3,2,1,0:T(8,128)S(1)} copy-done((f32[4,3,8,384]{3,2,1,0:T(8,128)S(1)}, f32[4,3,8,384]{3,2,1,0:T(8,128)}, u32[]{:S(2)}) %copy-start) | copy-done | bytes 147480
  12.3 0.0 copy-start.2
  12.3 0.0 copy-start.3
  12.3 0.7 %shard_map.78.refs_0_ = bf16[12,128,768]{2,1,0:T(8,128)(2,1)S(1)} custom-call(f32[4,3,8,384]{3,2,1,0:T(8,128)S(1)} %copy-done, f32[4,3,8,384]{3,2,1,0:T(8,128)S(1)} %collective-permute-done.refs_1_.refs_2_), custom_call_target="tpu_custom_call" | custom-call | tf_op jit(solution)/shard_map/pallas_call | solution.py:305
  13.0 4.6 %all-to-all-done = bf16[32,8,256]{2,1,0:T(8,128)(2,1)S(1)} async-done(((bf16[32,8,256]{2,1,0:T(8,128)(2,1)}), bf16[32,8,256]{2,1,0:T(8,128)(2,1)S(1)}, u32[]{:S(2)}, u32[]{:S(2)}) %all-to-all-start) | async-done | bytes 131104 | tf_op jit(solution)/shard_map/all_to_all | solution.py:281
  17.7 0.0 copy-done.4
  17.7 0.0 copy-done.1
  17.7 1.7 %shard_map.79 = bf16[2,128,256]{2,1,0:T(8,128)(2,1)S(1)} custom-call(bf16[4,4,256]{2,1,0:T(4,128)(2,1)S(1)} %copy-done.4, bf16[2,128,256]{2,1,0:T(8,128)(2,1)S(1)} %bitcast.13, bf16[12,128,768]{2,1,0:T(8,128)(2,1)S(1)} %shard_map.78.refs_0_, f32[4,3,8,384]{3,2,1,0:T(8,128)S(1)} %copy-done.1, f32[4,3,8,384]{3,2,1,0:T(8,128)S(1)} %collective-permute-done.refs_1_.refs_2_), custom_call_target="tpu_custom_call" | custom-call | tf_op jit(solution)/shard_map/pallas_call | solution.py:316
  19.4 9.9 %all_to_all.20 = bf16[32,8,256]{2,1,0:T(8,128)(2,1)S(1)} all-to-all(bf16[32,8,256]{2,1,0:T(8,128)(2,1)S(1)} %bitcast.17), channel_id=1, replica_groups=mesh['lon'=16,'lat'=2] {'lat','lon'}, dimensions={0} | all-to-all | bytes 262144 | tf_op jit(solution)/shard_map/all_to_all | solution.py:281
  29.3 0.0 copy-done.2
  29.3 0.0 copy-done.3
  29.3 1.0 %shard_map.80 = (bf16[256,256]{1,0:T(8,128)(2,1)}, bf16[256,256]{1,0:T(8,128)(2,1)S(1)}) custom-call(bf16[256,256]{1,0:T(8,128)(2,1)S(1)} %bitcast.14, bf16[256,256]{1,0:T(8,128)(2,1)S(1)} %copy-done.2, bf16[256,256]{1,0:T(8,128)(2,1)S(1)} %bitcast.19), custom_call_target="tpu_custom_call" | custom-call | tf_op jit(solution)/shard_map/pallas_call | solution.py:332
  30.3 9.9 %all_to_all.21 = bf16[32,8,256]{2,1,0:T(8,128)(2,1)S(1)} all-to-all(bf16[32,8,256]{2,1,0:T(8,128)(2,1)S(1)} %bitcast.20), channel_id=1, replica_groups=mesh['lon'=16,'lat'=2] {'lat','lon'}, dimensions={0} | all-to-all | bytes 262144 | tf_op jit(solution)/shard_map/all_to_all | solution.py:281
  40.2 2.1 %shard_map.81 = bf16[2,128,256]{2,1,0:T(8,128)(2,1)S(1)} custom-call(bf16[4,4,256]{2,1,0:T(4,128)(2,1)S(1)} %copy-done.4, bf16[2,128,256]{2,1,0:T(8,128)(2,1)S(1)} %bitcast.15, f32[4,3,8,384]{3,2,1,0:T(8,128)S(1)} %copy-done.1, f32[4,3,8,384]{3,2,1,0:T(8,128)S(1)} %collective-permute-done.refs_1_.refs_2_), custom_call_target="tpu_custom_call" | custom-call | tf_op jit(solution)/shard_map/pallas_call | solution.py:316
  42.4 9.9 %all_to_all.22 = bf16[32,8,256]{2,1,0:T(8,128)(2,1)S(1)} all-to-all(bf16[32,8,256]{2,1,0:T(8,128)(2,1)S(1)} %bitcast.16), channel_id=1, replica_groups=mesh['lon'=16,'lat'=2] {'lat','lon'}, dimensions={0} | all-to-all | bytes 262144 | tf_op jit(solution)/shard_map/all_to_all | solution.py:281
  52.3 0.7 %shard_map.82 = bf16[256,256]{1,0:T(8,128)(2,1)} custom-call(bf16[256,256]{1,0:T(8,128)(2,1)S(1)} %bitcast.18), custom_call_target="tpu_custom_call" | custom-call | tf_op jit(solution)/shard_map/pallas_call | solution.py:42
Async XLA Ops:
  0.6 17.0 %copy-start.4 = (bf16[4,4,256]{2,1,0:T(4,128)(2,1)S(1)}, bf16[4,4,256]{2,1,0:T(4,128)(2,1)}, u32[]{:S(2)}) copy-start(bf16[4,4,256]{2,1,0:T(4,128)(2,1)} %w_ref.7) | copy-start | bytes 24580
  2.4 15.2 %copy-start.1 = (f32[4,3,8,384]{3,2,1,0:T(8,128)S(1)}, f32[4,3,8,384]{3,2,1,0:T(8,128)}, u32[]{:S(2)}) copy-start(f32[4,3,8,384]{3,2,1,0:T(8,128)} %get-tuple-element.7.refs_0_.refs_1_) | copy-start | bytes 442372
  2.4 15.2 %all-to-all-start = ((bf16[32,8,256]{2,1,0:T(8,128)(2,1)}), bf16[32,8,256]{2,1,0:T(8,128)(2,1)S(1)}, u32[]{:S(2)}, u32[]{:S(2)}) async-start(bf16[32,8,256]{2,1,0:T(8,128)(2,1)} %bitcast.23), calls=%async_computation | async-start | bytes 262144 | tf_op jit(solution)/shard_map/all_to_all | solution.py:281
  9.7 1.6 %collective-permute-start = (f32[4,3,8,384]{3,2,1,0:T(8,128)}, f32[4,3,8,384]{3,2,1,0:T(8,128)S(1)}, u32[]{:S(2)}, u32[]{:S(2)}) collective-permute-start(f32[4,3,8,384]{3,2,1,0:T(8,128)} %get-tuple-element.7.refs_0_.refs_1_), channel_id=1, source_target_pairs={{0,1},{1,0},{2,3},{3,2},{4,5},{5,4},{6,7},{7,6},{8,9},{9,8},{10,11... | collective-permute-start | bytes 442376 | tf_op jit(solution)/shard_map/ppermute | solution.py:297
  11.4 0.9 %copy-start = (f32[4,3,8,384]{3,2,1,0:T(8,128)S(1)}, f32[4,3,8,384]{3,2,1,0:T(8,128)}, u32[]{:S(2)}) copy-start(f32[4,3,8,384]{3,2,1,0:T(8,128)} %get-tuple-element.7.refs_0_.refs_1_) | copy-start | bytes 442372
  12.3 17.0 %copy-start.2 = (bf16[256,256]{1,0:T(8,128)(2,1)S(1)}, bf16[256,256]{1,0:T(8,128)(2,1)}, u32[]{:S(2)}) copy-start(bf16[256,256]{1,0:T(8,128)(2,1)} %w_ref.6) | copy-start | bytes 393220
  12.3 17.0 %copy-start.3 = (bf16[8,32,256]{2,1,0:T(8,128)(2,1)S(1)}, bf16[8,32,256]{2,1,0:T(8,128)(2,1)}, u32[]{:S(2)}) copy-start(bf16[8,32,256]{2,1,0:T(8,128)(2,1)} %param.11) | copy-start | bytes 393220
